TPU v7x, 32 devices: a whole 2x2x4 slice. The times are simulated.
32 devices in a mesh: fsdp: 4 (over y, x), tensor: 8 (over z, core).
Axes of the slice: x: 2, y: 2, z: 4, core: 2. Of those that a mesh axis runs over, the one named last changes fastest.
Arguments:
- inputs: bfloat16 [768, 8192], P('fsdp'), may hold values from -6 to 6
- cotangent: bfloat16 [768, 8192], P('fsdp'), may hold values from -1.1953125 to 1.1953125
- up_tiles: bfloat16 [8, 16, 128, 128], P('tensor', 'fsdp'), may hold values from -0.75 to 0.75
- up_rows: int32 [8, 16], P('tensor', 'fsdp'), may hold values from 0 to 63, as said below
- up_cols: int32 [8, 16], P('tensor', 'fsdp'), may hold values from 0 to 31, as said below
- down_tiles: bfloat16 [8, 16, 128, 128], P('tensor', 'fsdp'), may hold values from -0.75 to 0.75
- down_rows: int32 [8, 16], P('tensor', 'fsdp'), may hold values from 0 to 31, as said below
- down_cols: int32 [8, 16], P('tensor', 'fsdp'), may hold values from 0 to 63, as said below
Outputs:
- input_grad: bfloat16 [768, 8192], P('fsdp', 'tensor')
- up_grad: bfloat16 [8, 16, 128, 128], P('tensor', 'fsdp')
- down_grad: bfloat16 [8, 16, 128, 128], P('tensor', 'fsdp')
Inputs may be any that keep to these rules, and one draw needn't show every extreme that they name: `up_rows`: together with up_cols, the positions of a group's 16 tiles are distinct; slot s is held by fsdp index s // 4. `up_cols`: see up_rows. `down_rows`: together with down_cols, the positions of a group's 16 tiles are distinct; slot s is held by fsdp index s // 4. `down_cols`: see down_rows.
All inputs are finite; a program needn't handle non-finite values.
Results may differ from a plain program's by a relative error of at most 0.015.
Values may be sent and summed in bfloat16 or wider, within the bound.
No kernel may reach another device: no remote copies, remote signals or barrier semaphores. Data moves between devices by JAX's collectives and lax.ppermute only.
A program may use at most 128 MiB of HBM per device.

v0:
```python
import jax
import jax.numpy as jnp
from jax import lax
from jax.sharding import PartitionSpec as P

FF = 32768
TILE = 128


def gelu_parts(pre):
    coef = 0.7978845608028654
    inner = coef * (pre + 0.044715 * pre * pre * pre)
    tanh_val = jnp.tanh(inner)
    act = 0.5 * pre * (1.0 + tanh_val)
    slope = 0.5 * (1.0 + tanh_val) + 0.5 * pre * (1.0 - tanh_val * tanh_val) * coef * (
        1.0 + 3.0 * 0.044715 * pre * pre
    )
    return (act, slope)


def on_device(inputs, cotangent, up_tiles, up_rows, up_cols, down_tiles, down_rows, down_cols):
    tok_count = inputs.shape[0]
    row_blocks = inputs.shape[1] // TILE
    group_cols = FF // (lax.axis_size("tensor") * TILE)
    input_blocks = inputs.reshape(tok_count, row_blocks, TILE)
    cotan_blocks = cotangent.reshape(tok_count, row_blocks, TILE)
    gathered = (
        lax.all_gather(up_tiles, "fsdp", axis=1, tiled=True),
        lax.all_gather(up_rows, "fsdp", axis=1, tiled=True),
        lax.all_gather(up_cols, "fsdp", axis=1, tiled=True),
        lax.all_gather(down_tiles, "fsdp", axis=1, tiled=True),
        lax.all_gather(down_rows, "fsdp", axis=1, tiled=True),
        lax.all_gather(down_cols, "fsdp", axis=1, tiled=True),
    )
    w_up, r_up, c_up = (gathered[0][0], gathered[1][0], gathered[2][0])
    w_down, r_down, c_down = (gathered[3][0], gathered[4][0], gathered[5][0])
    x_sel = jnp.take(input_blocks, r_up, axis=1)
    prod = jnp.einsum("tsk,skf->stf", x_sel, w_up, preferred_element_type=jnp.float32)
    pre = jax.ops.segment_sum(prod, c_up, num_segments=group_cols)
    act, slope = gelu_parts(pre)
    hidden = act.astype(jnp.bfloat16)
    dy_sel = jnp.take(cotan_blocks, c_down, axis=1)
    h_sel = jnp.take(hidden, r_down, axis=0)
    back = jnp.einsum("tsk,sfk->stf", dy_sel, w_down, preferred_element_type=jnp.float32)
    dhid = jax.ops.segment_sum(back, r_down, num_segments=group_cols)
    dpre = (dhid * slope).astype(jnp.bfloat16)
    dp_sel = jnp.take(dpre, c_up, axis=0)
    both_sum = lax.psum_scatter(
        jnp.stack(
            [
                jnp.einsum("tsk,stf->skf", x_sel, dp_sel, preferred_element_type=jnp.float32),
                jnp.einsum("stf,tsk->sfk", h_sel, dy_sel, preferred_element_type=jnp.float32),
            ],
            axis=1,
        ).astype(jnp.bfloat16),
        "fsdp",
        scatter_dimension=0,
        tiled=True,
    ).astype(jnp.float32)
    up_sum = both_sum[:, 0]
    down_sum = both_sum[:, 1]
    back_in = jnp.einsum("stf,skf->stk", dp_sel, w_up, preferred_element_type=jnp.float32)
    in_part = jax.ops.segment_sum(back_in, r_up, num_segments=row_blocks)
    own_blocks = lax.psum_scatter(
        in_part.astype(jnp.bfloat16), "tensor", scatter_dimension=0, tiled=True
    ).astype(jnp.float32)
    input_grad = jnp.transpose(own_blocks, (1, 0, 2)).reshape(tok_count, -1).astype(jnp.bfloat16)
    up_grad = up_sum.astype(jnp.bfloat16)[None]
    down_grad = down_sum.astype(jnp.bfloat16)[None]
    return (input_grad, up_grad, down_grad)


def solution(mesh):
    placed = (
        P("fsdp", None),
        P("fsdp", None),
        P("tensor", "fsdp", None, None),
        P("tensor", "fsdp"),
        P("tensor", "fsdp"),
        P("tensor", "fsdp", None, None),
        P("tensor", "fsdp"),
        P("tensor", "fsdp"),
    )
    return jax.shard_map(
        on_device,
        mesh=mesh,
        in_specs=placed,
        out_specs=(
            P("fsdp", "tensor"),
            P("tensor", "fsdp", None, None),
            P("tensor", "fsdp", None, None),
        ),
        check_vma=False,
    )
```

profile of v0, /device:TPU:0, one launch (start us, length us, event | category | flops | bytes accessed | tf_op | source)
XLA Modules:
  0.0 158.0 jit_solution(4273849891473987312)
XLA Ops:
  8.0 0.0 copy-start
  8.0 0.0 all-reduce.8.cloned.1.call-start
  8.1 1.4 fusion.27
  10.1 0.8 bitcast_dynamic-update-slice_fusion
  10.9 0.7 bitcast_dynamic-update-slice_fusion.1
  11.6 0.7 bitcast_dynamic-update-slice_fusion.3
  12.4 0.7 bitcast_dynamic-update-slice_fusion.2
  13.1 8.8 %all-reduce.5 = (s32[16]{0:T(128)S(1)}, s32[16]{0:T(128)S(1)}, s32[16]{0:T(128)S(1)}, s32[16]{0:T(128)S(1)}) all-reduce(s32[16]{0:T(128)S(1)} %bitcast_dynamic-update-slice_fusion.3, s32[16]{0:T(128)S(1)} %bitcast_dynamic-update-slice_fusion.1, s32[16]{0:T(128)S(1)} %bitcast_dynamic-update-slice_fusion, ...), channel_id=1, replica_groups=mesh['fsdp'=4,'tensor'=8] {'fsdp'}, use_global_device_ids=true, to_apply=%add | all-reduce | flops 64 | bytes 512 | tf_op jit(solution)/shard_map/broadcast_in_dim;squeeze | solution.py:63
  22.1 11.1 %all_gather.23 = bf16[1,16,128,128]{3,2,0,1:T(8,128)(2,1)} all-gather(bf16[1,4,128,128]{3,2,0,1:T(8,128)(2,1)} %bitcast.60), channel_id=1, replica_groups=mesh['fsdp'=4,'tensor'=8] {'fsdp'}, dimensions={1}, use_global_device_ids=true | all-gather | bytes 655360 | tf_op jit(solution)/shard_map/all_gather | solution.py:28
  33.1 10.8 %all_gather.21 = bf16[1,16,128,128]{3,2,0,1:T(8,128)(2,1)} all-gather(bf16[1,4,128,128]{3,2,0,1:T(8,128)(2,1)} %bitcast.61), channel_id=1, replica_groups=mesh['fsdp'=4,'tensor'=8] {'fsdp'}, dimensions={1}, use_global_device_ids=true | all-gather | bytes 655360 | tf_op jit(solution)/shard_map/all_gather | solution.py:31
  44.0 0.0 copy-done
  44.0 0.0 copy-start.1
  44.0 2.6 %copy_bitcast_fusion = bf16[192,64,128]{2,0,1:T(8,128)(2,1)} fusion(bf16[192,8192]{1,0:T(8,128)(2,1)S(1)} %copy-done), kind=kLoop, calls=%fused_computation.16 | loop fusion | bytes 6291456 | tf_op jit(solution)/shard_map/reshape | solution.py:25
  46.6 0.0 copy-done.1
  46.6 2.6 %copy_bitcast_fusion.1 = bf16[192,64,128]{2,0,1:T(8,128)(2,1)} fusion(bf16[192,8192]{1,0:T(8,128)(2,1)S(1)} %copy-done.1), kind=kLoop, calls=%fused_computation.17 | loop fusion | bytes 6291456 | tf_op jit(solution)/shard_map/reshape | solution.py:26
  49.1 3.4 %gather_fusion.1 = bf16[16,192,128]{2,1,0:T(8,128)(2,1)} fusion(bf16[192,64,128]{2,0,1:T(8,128)(2,1)} %copy_bitcast_fusion, s32[1024]{0:T(1024)S(1)} %pad_clamp_fusion.2), kind=kCustom, calls=%fused_computation.2.clone | custom fusion | bytes 1572928 | tf_op jit(solution)/shard_map/jit(_take)/gather | solution.py:37
  52.6 3.5 %gather_fusion = bf16[16,192,128]{2,1,0:T(8,128)(2,1)} fusion(bf16[192,64,128]{2,0,1:T(8,128)(2,1)} %copy_bitcast_fusion.1, s32[1024]{0:T(1024)S(1)} %pad_clamp_fusion.3), kind=kCustom, calls=%fused_computation.clone | custom fusion | bytes 1572928 | tf_op jit(solution)/shard_map/jit(_take)/gather | solution.py:42
  56.0 2.8 %fusion.10 = f32[16,192,128]{2,1,0:T(8,128)} fusion(bf16[1,16,128,128]{3,2,0,1:T(8,128)(2,1)} %all_gather.23, bf16[16,192,128]{2,1,0:T(8,128)(2,1)} %gather_fusion.1, pred[16]{0:T(512)(128)(4,1)S(1)} %get-tuple-element.18), kind=kOutput, calls=%fused_computation.25 | convolution fusion | flops 101056512 | bytes 2883600 | tf_op jit(solution)/shard_map/tsk,skf->stf/dot_general | solution.py:38
  58.9 2.0 %broadcast.38.clone = f32[32,192,128]{2,1,0:T(8,128)} broadcast(f32[]{:T(128)} %constant.22.clone.1), dimensions={} | broadcast | bytes 3145732 | tf_op jit(solution)/shard_map/broadcast.23
  60.9 4.5 %scatter_fusion.1 = f32[32,192,128]{2,1,0:T(8,128)} fusion(f32[32,192,128]{2,1,0:T(8,128)} %broadcast.38.clone, s32[16]{0:T(128)S(1)} %get-tuple-element.8, f32[16,192,128]{2,1,0:T(8,128)} %fusion.10), kind=kCustom, calls=%fused_computation.5 | custom fusion | flops 393216 | bytes 4718656 | tf_op jit(solution)/shard_map/scatter-add | solution.py:39
  65.4 2.9 %fusion.13 = f32[16,192,128]{2,1,0:T(8,128)} fusion(bf16[1,16,128,128]{3,2,0,1:T(8,128)(2,1)} %all_gather.21, bf16[16,192,128]{2,1,0:T(8,128)(2,1)} %gather_fusion, pred[16]{0:T(512)(128)(4,1)S(1)} %compare_and_fusion.3), kind=kOutput, calls=%fused_computation.28 | convolution fusion | flops 101056512 | bytes 2883600 | tf_op jit(solution)/shard_map/tsk,sfk->stf/dot_general | solution.py:44
  68.3 2.1 %broadcast.38.clone.1 = f32[32,192,128]{2,1,0:T(8,128)} broadcast(f32[]{:T(128)} %constant.22.clone.1), dimensions={} | broadcast | bytes 3145732 | tf_op jit(solution)/shard_map/broadcast.23
  70.4 4.5 %scatter_fusion = f32[32,192,128]{2,1,0:T(8,128)} fusion(f32[32,192,128]{2,1,0:T(8,128)} %broadcast.38.clone.1, s32[16]{0:T(128)S(1)} %get-tuple-element.6, f32[16,192,128]{2,1,0:T(8,128)} %fusion.13), kind=kCustom, calls=%fused_computation.4 | custom fusion | flops 393216 | bytes 4718656 | tf_op jit(solution)/shard_map/scatter-add | solution.py:45
  74.9 5.3 %multiply_convert_fusion = (bf16[32,192,128]{2,1,0:T(8,128)(2,1)}, bf16[32,192,128]{2,1,0:T(8,128)(2,1)}) fusion(f32[32,192,128]{2,1,0:T(8,128)} %scatter_fusion.1, f32[32,192,128]{2,1,0:T(8,128)} %scatter_fusion), kind=kLoop, calls=%fused_computation.18 | loop fusion | flops 16515072 | bytes 9437184 | tf_op jit(solution)/shard_map/convert_element_type | solution.py:41
  80.2 2.9 %gather_fusion.3 = bf16[16,192,128]{2,1,0:T(8,128)(2,1)} fusion(bf16[32,192,128]{2,1,0:T(8,128)(2,1)} %get-tuple-element.9, s32[1024]{0:T(1024)S(1)} %pad_clamp_fusion), kind=kCustom, calls=%fused_computation.3.clone | custom fusion | bytes 1572928 | tf_op jit(solution)/shard_map/jit(_take)/gather | solution.py:43
  83.1 2.8 %fusion.8 = bf16[16,1,128,128]{3,2,0,1:T(8,128)(2,1)} fusion(bf16[16,192,128]{2,1,0:T(8,128)(2,1)} %gather_fusion.3, pred[16]{0:T(512)(128)(4,1)S(1)} %compare_and_fusion, bf16[16,192,128]{2,1,0:T(8,128)(2,1)} %gather_fusion, pred[16]{0:T(512)(128)(4,1)S(1)} %compare_and_fusion.3), kind=kOutput, calls=%fused_computation.22 | convolution fusion | flops 101711872 | bytes 2097184 | tf_op jit(solution)/shard_map/stf,tsk->sfk/dot_general | solution.py:52
  85.9 3.0 %gather_fusion.2 = bf16[16,192,128]{2,1,0:T(8,128)(2,1)} fusion(bf16[32,192,128]{2,1,0:T(8,128)(2,1)} %get-tuple-element.10, s32[1024]{0:T(1024)S(1)} %pad_clamp_fusion.1), kind=kCustom, calls=%fused_computation.1.clone | custom fusion | bytes 1572928 | tf_op jit(solution)/shard_map/jit(_take)/gather | solution.py:47
  88.9 0.0 copy-start.2
  88.9 2.0 %fusion.7 = bf16[16,1,128,128]{3,2,0,1:T(8,128)(2,1)S(1)} fusion(bf16[16,192,128]{2,1,0:T(8,128)(2,1)} %gather_fusion.1, pred[16]{0:T(512)(128)(4,1)S(1)} %get-tuple-element.18, bf16[16,192,128]{2,1,0:T(8,128)(2,1)} %gather_fusion.2, pred[16]{0:T(512)(128)(4,1)S(1)} %get-tuple-element.17), kind=kOutput, calls=%fused_computation.21 | convolution fusion | flops 101711872 | bytes 2097184 | tf_op jit(solution)/shard_map/tsk,stf->skf/dot_general | solution.py:51
  90.9 0.0 copy-done.2
  90.9 1.1 pad_maximum_fusion
  92.0 0.0 all-reduce.8.cloned.1.call-update
  92.0 0.0 reduce-scatter.5.cloned.1.call-start
  92.0 2.9 %fusion.17 = f32[16,192,128]{2,1,0:T(8,128)} fusion(bf16[1,16,128,128]{3,2,0,1:T(8,128)(2,1)} %all_gather.23, bf16[16,192,128]{2,1,0:T(8,128)(2,1)} %gather_fusion.2, pred[16]{0:T(512)(128)(4,1)S(1)} %get-tuple-element.17), kind=kOutput, calls=%fused_computation.35 | convolution fusion | flops 101056512 | bytes 2883600 | tf_op jit(solution)/shard_map/stf,skf->stk/dot_general | solution.py:62
  95.0 3.4 %broadcast_in_dim.23 = f32[64,192,128]{2,1,0:T(8,128)} broadcast(f32[]{:T(128)} %constant.22.clone.1), dimensions={} | broadcast | bytes 6291460 | tf_op jit(solution)/shard_map/broadcast_in_dim | solution.py:63
  98.4 4.6 %scatter_fusion.2 = f32[64,192,128]{2,1,0:T(8,128)} fusion(f32[64,192,128]{2,1,0:T(8,128)} %broadcast_in_dim.23, s32[16]{0:T(128)S(1)} %get-tuple-element.5, f32[16,192,128]{2,1,0:T(8,128)} %fusion.17), kind=kCustom, calls=%fused_computation.6 | custom fusion | flops 393216 | bytes 4718656 | tf_op jit(solution)/shard_map/scatter-add | solution.py:63
  103.0 5.1 %convert_element_type.42 = bf16[64,192,128]{2,1,0:T(8,128)(2,1)} convert(f32[64,192,128]{2,1,0:T(8,128)} %scatter_fusion.2) | non-fusion elementwise | flops 1572864 | bytes 9437184 | tf_op jit(solution)/shard_map/convert_element_type | solution.py:65
  108.1 0.0 reduce-scatter.5.cloned.1.call-update
  108.7 36.3 %all-reduce.8.cloned.1.call-done = bf16[16,2,128,128]{3,2,0,1:T(8,128)(2,1)} async-done(((bf16[16,2,128,128]{3,2,0,1:T(8,128)(2,1)}), bf16[16,2,128,128]{3,2,0,1:T(8,128)(2,1)}) %all-reduce.8.cloned.1.call-update) | async-done | bytes 1048592
  145.1 1.7 %dynamic-slice_bitcast_fusion = (bf16[1,4,128,128]{3,2,1,0:T(8,128)(2,1)}, bf16[1,4,128,128]{3,2,1,0:T(8,128)(2,1)}) fusion(bf16[16,2,128,128]{3,2,0,1:T(8,128)(2,1)} %all-reduce.8.cloned.1.call-done, u32[]{:T(128)S(6)} %multiply.13, u32[]{:T(128)S(6)} %convert.16), kind=kLoop, calls=%fused_computation.41 | loop fusion | bytes 524296 | tf_op jit(solution)/shard_map/convert_element_type | solution.py:69
  146.8 2.0 %reduce-scatter.5.cloned.1.call-done = bf16[8,192,128]{2,1,0:T(8,128)(2,1)} async-done(((bf16[64,192,128]{2,1,0:T(8,128)(2,1)}), bf16[8,192,128]{2,1,0:T(8,128)(2,1)}) %reduce-scatter.5.cloned.1.call-update) | async-done | bytes 393232 | tf_op jit(solution)/shard_map/reduce_scatter | solution.py:64
  148.7 1.8 %copy_bitcast_fusion.2 = bf16[192,1024]{1,0:T(8,128)(2,1)} fusion(bf16[8,192,128]{2,1,0:T(8,128)(2,1)} %reduce-scatter.5.cloned.1.call-done), kind=kLoop, calls=%fused_computation.39 | loop fusion | bytes 786432 | tf_op jit(solution)/shard_map/convert_element_type | solution.py:67
  (14 shorter events, 0.1 us)
Async XLA Ops:
  8.0 36.0 %copy-start = (bf16[192,8192]{1,0:T(8,128)(2,1)S(1)}, bf16[192,8192]{1,0:T(8,128)(2,1)}, u32[]{:S(2)}) copy-start(bf16[192,8192]{1,0:T(8,128)(2,1)} %param.12) | copy-start | bytes 9437188
  8.0 137.0 %all-reduce.8.cloned.1.call-start = ((), (), s32[]{:S(2)}) async-start(), calls=%async_computation.2 | async-start | bytes 2097152
  44.0 2.6 %copy-start.1 = (bf16[192,8192]{1,0:T(8,128)(2,1)S(1)}, bf16[192,8192]{1,0:T(8,128)(2,1)}, u32[]{:S(2)}) copy-start(bf16[192,8192]{1,0:T(8,128)(2,1)} %param.13) | copy-start | bytes 9437188
  88.9 2.0 %copy-start.2 = (bf16[16,1,128,128]{3,2,0,1:T(8,128)(2,1)S(1)}, bf16[16,1,128,128]{3,2,0,1:T(8,128)(2,1)}, u32[]{:S(2)}) copy-start(bf16[16,1,128,128]{3,2,0,1:T(8,128)(2,1)} %fusion.8) | copy-start | bytes 1572868
  92.0 56.7 %reduce-scatter.5.cloned.1.call-start = ((), (), s32[]{:S(2)}) async-start(), calls=%async_computation.1 | async-start | bytes 3538944 | tf_op jit(solution)/shard_map/reduce_scatter | solution.py:64
Sparse Core Ops, SparseCore 0:
  92.1 52.9 all-reduce.7
Sparse Core Ops, SparseCore 1:
  108.2 40.5 reduce-scatter.4
where the time goes:
time: 159 us; the launch traced here: 158 us
  waiting for transfers between devices  38.3 us (24%)
  local copies, waits for them, and re-layouts  33.4 us (21%)
  blocking collectives  30.7 us (19%)
  other arithmetic  25.1 us (16%)
  between operations  16.9 us (11%)
  matrix products  13.5 us (8%)
    unnamed x3, waiting for transfers between devices  36.4 us
    all_gather x1, blocking collectives, on_device(): lax.all_gather(up_tiles, 'fsdp', axis=1, tiled=True)  11.1 us
    all_gather x1, blocking collectives, on_device(): lax.all_gather(down_tiles, 'fsdp', axis=1, tiled=True)  10.8 us
    another operation x1, blocking collectives, on_device(): in_part = jax.ops.segment_sum(back_in, r_up, num_segments=row_blocks)  8.82 us
    convert_element_type x1, other arithmetic, on_device(): hidden = act.astype(jnp.bfloat16)  5.3 us
    convert_element_type x1, other arithmetic, on_device(): in_part.astype(jnp.bfloat16)  5.11 us
    scatter-add x1, other arithmetic, on_device(): in_part = jax.ops.segment_sum(back_in, r_up, num_segments=row_blocks)  4.55 us
    scatter-add x1, other arithmetic, on_device(): dhid = jax.ops.segment_sum(back, r_down, num_segments=group_cols)  4.5 us
  transfers between devices with their start and end apart: 2, of which 2 were waited for; matrix products, arithmetic and copies ran while one was open for 11% of the time, Pallas kernels for 0%

commit v1 on v0

v1 whole, which is shorter than its diff:
```python
import functools

import jax
import jax.numpy as jnp
from jax import lax
from jax.experimental import pallas as pl
from jax.experimental.pallas import tpu as pltpu
from jax.sharding import PartitionSpec as P

FF = 32768
TILE = 128
IDX_ROWS = 16
BF16 = jnp.bfloat16
F32 = jnp.float32

VMEM = pl.BlockSpec(memory_space=pltpu.VMEM)
SMEM = pl.BlockSpec(memory_space=pltpu.SMEM)
ANY = pl.BlockSpec(memory_space=pl.ANY)


def gelu_parts(pre):
    coef = 0.7978845608028654
    sq = pre * pre
    tanh_val = jnp.tanh(coef * (pre + 0.044715 * pre * sq))
    half = 0.5 * (1.0 + tanh_val)
    act = pre * half
    slope = half + 0.5 * pre * (1.0 - tanh_val * tanh_val) * coef * (
        1.0 + 3.0 * 0.044715 * sq
    )
    return (act, slope)


def pack_kernel(up_ref, down_ref, ur_ref, uc_ref, dr_ref, dc_ref, out_ref):
    held = up_ref.shape[0] // TILE
    rows = up_ref.shape[0]
    out_ref[:rows] = up_ref[...]
    out_ref[rows : 2 * rows] = down_ref[...]
    lane = lax.broadcasted_iota(jnp.int32, (IDX_ROWS, TILE), 1)
    val = jnp.zeros((IDX_ROWS, TILE), jnp.int32)
    for kind, ref in enumerate((ur_ref, uc_ref, dr_ref, dc_ref)):
        for i in range(held):
            val = jnp.where(lane == kind * held + i, ref[0, i], val)
    out_ref[2 * rows :] = val.astype(F32).astype(BF16)


def dot(a, b, dims):
    return lax.dot_general(a, b, (dims, ((), ())), preferred_element_type=F32)


def main_kernel(n_f, held, n_z, per_dev, z_ref, x_ref, dy_ref, *refs):
    packs = refs[:n_f]
    mine = refs[n_f : n_f + n_z]
    other = refs[n_f + n_z : n_f + 2 * n_z]
    xs, dys, dps, hs = refs[n_f + 2 * n_z : n_f + 2 * n_z + 4]
    pre, dhid, hid, dpre, acc, idx_v, idx, flag, sem_i, sem_x, sem_y = refs[
        n_f + 2 * n_z + 4 :
    ]
    slots = n_f * held
    rows = held * TILE
    z, core = z_ref[0], z_ref[1]
    for f in range(n_f):
        idx_v[f : f + 1] = packs[f][2 * rows :][:1].astype(F32).astype(jnp.int32)
    copy = pltpu.make_async_copy(idx_v, idx, sem_i)
    copy.start()
    copy.wait()

    def at(kind, s):
        return idx[s // held, kind * held + s % held]

    def block(ref, which, out, sem, s):
        col = pl.ds(pl.multiple_of(which * TILE, TILE), TILE)
        return pltpu.make_async_copy(ref.at[:, col], out.at[s], sem.at[s])

    for s in range(slots):
        block(x_ref, at(0, s), xs, sem_x, s).start()
        block(dy_ref, at(3, s), dys, sem_y, s).start()
    pre[...] = jnp.zeros_like(pre)
    dhid[...] = jnp.zeros_like(dhid)
    hid[...] = jnp.zeros_like(hid)
    acc[...] = jnp.zeros_like(acc)
    for c in range(pre.shape[0]):
        flag[c] = 0

    def up_tile(s):
        return packs[s // held][pl.ds((s % held) * TILE, TILE)]

    def down_tile(s):
        return packs[s // held][pl.ds(rows + (s % held) * TILE, TILE)]

    for s in range(slots):
        block(x_ref, at(0, s), xs, sem_x, s).wait()
        pre[at(1, s)] += dot(xs[s], up_tile(s), ((1,), (0,)))
    for s in range(slots):
        block(dy_ref, at(3, s), dys, sem_y, s).wait()
        dhid[at(2, s)] += dot(dys[s], down_tile(s), ((1,), (1,)))
    for s in range(slots):
        c = at(1, s)

        @pl.when(flag[c] == 0)
        def _():
            act, slope = gelu_parts(pre[c])
            hid[c] = act.astype(BF16)
            dpre[c] = (dhid[c] * slope).astype(BF16)
            flag[c] = 1

    for s in range(slots):
        dp = dpre[at(1, s)]
        dps[s] = dp
        hs[s] = hid[at(2, s)]
        r = at(0, s)
        dev, j = r // per_dev, r % per_dev
        to_z, to_core = dev // 2, dev % 2
        k = jnp.bitwise_xor(to_z, z) if n_z == 4 else to_z
        whose = jnp.bitwise_xor(to_core, core)
        col = pl.ds(pl.multiple_of(j * TILE, TILE), TILE)
        acc[whose * n_z + k, :, col] += dot(dp, up_tile(s), ((1,), (1,)))
    for k in range(n_z):
        mine[k][...] = acc[k].astype(BF16)
        other[k][...] = acc[n_z + k].astype(BF16)


def grad_kernel(n_f, held, xs, dys, dps, hs, *outs):
    for s in range(n_f * held):
        f, i = s // held, s % held
        outs[f][i] = dot(xs[s], dps[s], ((0,), (0,))).astype(BF16)
        outs[f][held + i] = dot(hs[s], dys[s], ((0,), (0,))).astype(BF16)


def vmem_limit(mb):
    return pltpu.CompilerParams(vmem_limit_bytes=mb * 1024 * 1024)


def on_device(inputs, cotangent, up_tiles, up_rows, up_cols, down_tiles, down_rows, down_cols):
    n_f, n_t = lax.axis_size("fsdp"), lax.axis_size("tensor")
    n_z = n_t // 2
    tok, width = inputs.shape
    per_dev = width // (n_t * TILE)
    group_cols = FF // (n_t * TILE)
    held = up_tiles.shape[1]
    rows = held * TILE
    slots = held * n_f
    t = lax.axis_index("tensor")
    z, core = t // 2, t % 2

    def over_f(a, k):
        return lax.ppermute(a, "fsdp", [(f, f ^ k) for f in range(n_f)])

    def over_t(a, k):
        return lax.ppermute(a, "tensor", [(i, i ^ k) for i in range(n_t)])

    pack = pl.pallas_call(
        pack_kernel,
        out_shape=jax.ShapeDtypeStruct((2 * rows + IDX_ROWS, TILE), BF16),
        in_specs=[VMEM, VMEM, SMEM, SMEM, SMEM, SMEM],
        out_specs=VMEM,
    )(
        up_tiles.reshape(rows, TILE),
        down_tiles.reshape(rows, TILE),
        up_rows,
        up_cols,
        down_rows,
        down_cols,
    )
    packs = [pack] + [over_f(pack, k) for k in range(1, n_f)]
    shard = jax.ShapeDtypeStruct((tok, per_dev * TILE), BF16)
    sel = jax.ShapeDtypeStruct((slots, tok, TILE), BF16)
    outs = pl.pallas_call(
        functools.partial(main_kernel, n_f, held, n_z, per_dev),
        out_shape=[shard] * (2 * n_z) + [sel] * 4,
        in_specs=[SMEM, ANY, ANY] + [VMEM] * n_f,
        out_specs=[VMEM] * (2 * n_z + 4),
        scratch_shapes=[
            pltpu.VMEM((group_cols, tok, TILE), F32),
            pltpu.VMEM((group_cols, tok, TILE), F32),
            pltpu.VMEM((group_cols, tok, TILE), BF16),
            pltpu.VMEM((group_cols, tok, TILE), BF16),
            pltpu.VMEM((2 * n_z, tok, per_dev * TILE), F32),
            pltpu.VMEM((n_f, TILE), jnp.int32),
            pltpu.SMEM((n_f, TILE), jnp.int32),
            pltpu.SMEM((group_cols,), jnp.int32),
            pltpu.SemaphoreType.DMA,
            pltpu.SemaphoreType.DMA((slots,)),
            pltpu.SemaphoreType.DMA((slots,)),
        ],
        compiler_params=vmem_limit(48),
    )(jnp.stack([z, core]).astype(jnp.int32), inputs, cotangent, *packs)
    mine, other = outs[:n_z], outs[n_z : 2 * n_z]
    chosen = outs[2 * n_z :]
    parts = [
        (m.astype(F32) + over_t(o, 1).astype(F32)).astype(BF16) for m, o in zip(mine, other)
    ]
    terms = pl.pallas_call(
        functools.partial(grad_kernel, n_f, held),
        out_shape=[jax.ShapeDtypeStruct((2 * held, TILE, TILE), BF16)] * n_f,
        in_specs=[VMEM] * 4,
        out_specs=[VMEM] * n_f,
        compiler_params=vmem_limit(48),
    )(*chosen)
    total = terms[0].astype(F32)
    for k in range(1, n_f):
        total = total + over_f(terms[k], k).astype(F32)
    total = total.astype(BF16)
    if n_z == 4:
        got = [parts[0]] + [over_t(parts[k], 2 * k) for k in range(n_z - 1, 0, -1)]
        input_grad = sum(g.astype(F32) for g in got).astype(BF16)
    else:
        input_grad = lax.psum_scatter(
            jnp.stack(parts),
            "tensor",
            scatter_dimension=0,
            tiled=False,
            axis_index_groups=[list(range(c, n_t, 2)) for c in range(2)],
        )
    return (input_grad, total[:held][None], total[held:][None])


def solution(mesh):
    placed = (
        P("fsdp", None),
        P("fsdp", None),
        P("tensor", "fsdp", None, None),
        P("tensor", "fsdp"),
        P("tensor", "fsdp"),
        P("tensor", "fsdp", None, None),
        P("tensor", "fsdp"),
        P("tensor", "fsdp"),
    )
    return jax.shard_map(
        on_device,
        mesh=mesh,
        in_specs=placed,
        out_specs=(
            P("fsdp", "tensor"),
            P("tensor", "fsdp", None, None),
            P("tensor", "fsdp", None, None),
        ),
        check_vma=False,
    )
```

time: 159 us -> 76.6 us (0.48)
  blocking collectives: 30.7 us -> 0 us
  local copies, waits for them, and re-layouts: 33.4 us -> 3.94 us
  other arithmetic: 25.1 us -> 1.69 us
  starting transfers between devices: 0.08 us -> 16.8 us
  between operations: 16.9 us -> 0.71 us
  matrix products: 13.5 us -> 0 us
  Pallas kernels: 0 us -> 13.2 us
  waiting for transfers between devices: 38.3 us -> 39.9 us
    ppermute x0 -> x13, waiting for transfers between devices: none -> 39.9 us  [the longest x7 22.9 us: over_t(): return lax.ppermute(a, 'tensor', [(i, i ^ k) for i in range(n_t)])]
    unnamed x3 -> x0, waiting for transfers between devices: 36.4 us -> none
    all_gather x2 -> x0, blocking collectives: 21.9 us -> none  [the longest x1 11.1 us: on_device(): lax.all_gather(up_tiles, 'fsdp', axis=1, tiled=True)]
    ppermute x0 -> x13, starting transfers between devices: none -> 16.8 us  [the longest x7 8.72 us: over_t(): return lax.ppermute(a, 'tensor', [(i, i ^ k) for i in range(n_t)])]
    scatter-add x3 -> x0, other arithmetic: 13.5 us -> none  [the longest x1 4.55 us: on_device(): in_part = jax.ops.segment_sum(back_in, r_up, num_segments=row_blocks)]
    dot_general x5 -> x0, matrix products: 13.5 us -> none  [the longest x1 2.94 us: on_device(): jnp.einsum('stf,skf->stk', dp_sel, w_up, preferred_element_type=jnp.float32)]
    pallas_call x0 -> x3, Pallas kernels: none -> 13.2 us  [the longest x1 10.8 us: on_device(): pl.pallas_call(functools.partial(main_kernel, n_f, held, n_z, per_dev), o...]
    gather x4 -> x0, local copies, waits for them, and re-layouts: 12.8 us -> none  [the longest x1 3.45 us: on_device(): dy_sel = jnp.take(cotan_blocks, c_down, axis=1)]
  transfers between devices with their start and end apart: 2 -> 13, of which waited for: 2 -> 7; matrix products, arithmetic and copies ran while one was open for 11% -> 2% of each run, Pallas kernels for 0% -> 1%
where the time goes in v1:
time: 76.6 us; the launch traced here: 76.3 us
  waiting for transfers between devices  39.9 us (52%)
  starting transfers between devices  16.8 us (22%)
  Pallas kernels  13.2 us (17%)
  local copies, waits for them, and re-layouts  3.94 us (5%)
  other arithmetic  1.69 us (2%)
    ppermute x7, waiting for transfers between devices, over_t(): return lax.ppermute(a, 'tensor', [(i, i ^ k) for i in range(n_t)])  22.9 us
    ppermute x6, waiting for transfers between devices, over_f(): return lax.ppermute(a, 'fsdp', [(f, f ^ k) for f in range(n_f)])  17 us
    pallas_call x1, Pallas kernels, on_device(): pl.pallas_call(functools.partial(main_kernel, n_f, held, n_z, per_dev), o...  10.8 us
    ppermute x7, starting transfers between devices, over_t(): return lax.ppermute(a, 'tensor', [(i, i ^ k) for i in range(n_t)])  8.72 us
    ppermute x6, starting transfers between devices, over_f(): return lax.ppermute(a, 'fsdp', [(f, f ^ k) for f in range(n_f)])  8.08 us
    unnamed x6, local copies, waits for them, and re-layouts  3.22 us
    pallas_call x1, Pallas kernels, on_device(): pl.pallas_call(pack_kernel, out_shape=jax.ShapeDtypeStruct((2 * rows + ID...  1.71 us
  transfers between devices with their start and end apart: 13, of which 7 were waited for; matrix products, arithmetic and copies ran while one was open for 2% of the time, Pallas kernels for 1%

profile of v1, /device:TPU:0, one launch (start us, length us, event | category | flops | bytes accessed | tf_op | source)
XLA Modules:
  0.0 76.3 jit_solution(3407810967681889066)
XLA Ops:
  0.6 1.7 %shard_map.103.refs_0_ = bf16[1040,128]{1,0:T(8,128)(2,1)} custom-call(bf16[512,128]{1,0:T(8,128)(2,1)} %bitcast.8, bf16[512,128]{1,0:T(8,128)(2,1)} %bitcast.9, s32[1,4]{1,0:T(1,128)} %ur_ref.1, s32[1,4]{1,0:T(1,128)} %uc_ref.1, s32[1,4]{1,0:T(1,128)} %dr_ref.1, s32[1,4]{1,0:T(1,128)} %dc_ref.1), custom_call_target="tpu_custom_call" | custom-call | tf_op jit(solution)/shard_map/pallas_call | solution.py:151
  2.3 3.9 %collective-permute-start.2 = (bf16[1040,128]{1,0:T(8,128)(2,1)}, bf16[1040,128]{1,0:T(8,128)(2,1)S(1)}, u32[]{:S(2)}, u32[]{:S(2)}) collective-permute-start(bf16[1040,128]{1,0:T(8,128)(2,1)} %shard_map.103.refs_0_), channel_id=1, source_target_pairs={{0,24},{8,16},{16,8},{24,0},{1,25},{9,17},{17,9},{25,1},{2,26},{10... | collective-permute-start | bytes 798728 | tf_op jit(solution)/shard_map/ppermute | solution.py:146
  6.2 0.5 collective-permute-start.1
  6.7 0.1 collective-permute-start
  6.8 0.1 pad_add_fusion.z_ref
  6.9 6.8 %collective-permute-done.2.refs_3_ = bf16[1040,128]{1,0:T(8,128)(2,1)S(1)} collective-permute-done((bf16[1040,128]{1,0:T(8,128)(2,1)}, bf16[1040,128]{1,0:T(8,128)(2,1)S(1)}, u32[]{:S(2)}, u32[]{:S(2)}) %collective-permute-start.2) | collective-permute-done | bytes 266272 | tf_op jit(solution)/shard_map/ppermute | solution.py:146
  13.7 4.8 %collective-permute-done.1.refs_2_ = bf16[1040,128]{1,0:T(8,128)(2,1)S(1)} collective-permute-done((bf16[1040,128]{1,0:T(8,128)(2,1)}, bf16[1040,128]{1,0:T(8,128)(2,1)S(1)}, u32[]{:S(2)}, u32[]{:S(2)}) %collective-permute-start.1) | collective-permute-done | bytes 266272 | tf_op jit(solution)/shard_map/ppermute | solution.py:146
  18.5 0.3 collective-permute-done.refs_1_
  18.8 0.0 copy-start
  18.8 0.9 %copy-done = bf16[1040,128]{1,0:T(8,128)(2,1)S(1)} copy-done((bf16[1040,128]{1,0:T(8,128)(2,1)S(1)}, bf16[1040,128]{1,0:T(8,128)(2,1)}, u32[]{:S(2)}) %copy-start) | copy-done | bytes 266264
  19.8 10.8 %shard_map.104 = (bf16[192,1024]{1,0:T(8,128)(2,1)S(1)}, bf16[192,1024]{1,0:T(8,128)(2,1)S(1)}, bf16[192,1024]{1,0:T(8,128)(2,1)S(1)}, bf16[192,1024]{1,0:T(8,12...) custom-call(s32[2]{0:T(128)S(1)} %pad_add_fusion.z_ref, ...), custom_call_target="tpu_custom_call" | custom-call | tf_op jit(solution)/shard_map/pallas_call | solution.py:167
  30.6 0.1 collective-permute-start.4
  30.6 0.5 collective-permute-start.6
  31.1 0.1 collective-permute-start.3
  31.2 0.4 collective-permute-start.8
  31.7 0.0 copy-start.1
  31.7 1.1 %copy-done.1 = bf16[16,192,128]{2,1,0:T(8,128)(2,1)S(1)} copy-done((bf16[16,192,128]{2,1,0:T(8,128)(2,1)S(1)}, bf16[16,192,128]{2,1,0:T(8,128)(2,1)}, u32[]{:S(2)}) %copy-start.1) | copy-done | bytes 786456
  32.8 0.0 copy-start.2
  32.8 1.1 %copy-done.2 = bf16[16,192,128]{2,1,0:T(8,128)(2,1)S(1)} copy-done((bf16[16,192,128]{2,1,0:T(8,128)(2,1)S(1)}, bf16[16,192,128]{2,1,0:T(8,128)(2,1)}, u32[]{:S(2)}) %copy-start.2) | copy-done | bytes 786456
  33.9 0.8 %shard_map.105 = (bf16[8,128,128]{2,1,0:T(8,128)(2,1)S(1)}, bf16[8,128,128]{2,1,0:T(8,128)(2,1)S(1)}, bf16[8,128,128]{2,1,0:T(8,128)(2,1)S(1)}, bf16[8,128,128]{2,1,0:T(8,128)(2,1)S(1)}) custom-call(bf16[16,192,128]{2,1,0:T(8,128)(2,1)S(1)} %get-tuple-element.27.xs, bf16[16,192,128]{2,1,0:T(8,128)(2,1)S(1)} %get-tuple-element.28.dys, ...), custom_call_target="tpu_custom_call" | custom-call | tf_op jit(solution)/shard_map/pallas_call | solution.py:192
  34.7 1.6 %collective-permute-start.10 = (bf16[8,128,128]{2,1,0:T(8,128)(2,1)S(1)}, bf16[8,128,128]{2,1,0:T(8,128)(2,1)S(1)}, u32[]{:S(2)}, u32[]{:S(2)}) collective-permute-start(bf16[8,128,128]{2,1,0:T(8,128)(2,1)S(1)} %get-tuple-element.32), channel_id=1, source_target_pairs={{0,8},{8,0},{16,24},{24,16},{1,9},{9,1},{17,25},{25,17},{2,10},{10... | collective-permute-start | bytes 786440 | tf_op jit(solution)/shard_map/ppermute | solution.py:146
  36.3 0.0 collective-permute-done.4
  36.3 0.5 collective-permute-start.11
  36.8 0.1 add_convert_fusion.3
  36.9 0.0 collective-permute-done.6
  36.9 1.5 %collective-permute-start.12 = (bf16[8,128,128]{2,1,0:T(8,128)(2,1)S(1)}, bf16[8,128,128]{2,1,0:T(8,128)(2,1)S(1)}, u32[]{:S(2)}, u32[]{:S(2)}) collective-permute-start(bf16[8,128,128]{2,1,0:T(8,128)(2,1)S(1)} %get-tuple-element.34), channel_id=1, source_target_pairs={{0,24},{8,16},{16,8},{24,0},{1,25},{9,17},{17,9},{25,1},{2,26},{10... | collective-permute-start | bytes 786440 | tf_op jit(solution)/shard_map/ppermute | solution.py:146
  38.5 0.1 add_convert_fusion.2
  38.6 0.0 collective-permute-done.8
  38.6 3.7 %collective-permute-start.5 = (bf16[192,1024]{1,0:T(8,128)(2,1)S(1)}, bf16[192,1024]{1,0:T(8,128)(2,1)S(1)}, u32[]{:S(2)}, u32[]{:S(2)}) collective-permute-start(bf16[192,1024]{1,0:T(8,128)(2,1)S(1)} %add_convert_fusion.3), channel_id=1, source_target_pairs={{0,6},{1,7},{2,4},{3,5},{4,2},{5,3},{6,0},{7,1},{8,14},{9,15},{10,... | collective-permute-start | bytes 1179656 | tf_op jit(solution)/shard_map/ppermute | solution.py:149
  42.3 0.1 add_convert_fusion.1
  42.4 1.5 %collective-permute-done.10 = bf16[8,128,128]{2,1,0:T(8,128)(2,1)S(1)} collective-permute-done((bf16[8,128,128]{2,1,0:T(8,128)(2,1)S(1)}, bf16[8,128,128]{2,1,0:T(8,128)(2,1)S(1)}, u32[]{:S(2)}, u32[]{:S(2)}) %collective-permute-start.10) | collective-permute-done | bytes 262176 | tf_op jit(solution)/shard_map/ppermute | solution.py:146
  43.9 2.5 %collective-permute-start.7 = (bf16[192,1024]{1,0:T(8,128)(2,1)S(1)}, bf16[192,1024]{1,0:T(8,128)(2,1)S(1)}, u32[]{:S(2)}, u32[]{:S(2)}) collective-permute-start(bf16[192,1024]{1,0:T(8,128)(2,1)S(1)} %add_convert_fusion.2), channel_id=1, source_target_pairs={{0,4},{1,5},{2,6},{3,7},{4,0},{5,1},{6,2},{7,3},{8,12},{9,13},{10,... | collective-permute-start | bytes 1179656 | tf_op jit(solution)/shard_map/ppermute | solution.py:149
  46.4 3.5 %collective-permute-done.11 = bf16[8,128,128]{2,1,0:T(8,128)(2,1)S(1)} collective-permute-done((bf16[8,128,128]{2,1,0:T(8,128)(2,1)S(1)}, bf16[8,128,128]{2,1,0:T(8,128)(2,1)S(1)}, u32[]{:S(2)}, u32[]{:S(2)}) %collective-permute-start.11) | collective-permute-done | bytes 262176 | tf_op jit(solution)/shard_map/ppermute | solution.py:146
  49.9 1.5 %collective-permute-start.9 = (bf16[192,1024]{1,0:T(8,128)(2,1)S(1)}, bf16[192,1024]{1,0:T(8,128)(2,1)S(1)}, u32[]{:S(2)}, u32[]{:S(2)}) collective-permute-start(bf16[192,1024]{1,0:T(8,128)(2,1)S(1)} %add_convert_fusion.1), channel_id=1, source_target_pairs={{0,2},{1,3},{2,0},{3,1},{4,6},{5,7},{6,4},{7,5},{8,10},{9,11},{10,... | collective-permute-start | bytes 1179656 | tf_op jit(solution)/shard_map/ppermute | solution.py:149
  51.4 0.0 collective-permute-done.12
  51.4 0.1 add_convert_fusion.5
  51.6 0.7 slice_bitcast_fusion
  52.3 0.0 collective-permute-done.3
  52.3 0.4 collective-permute-done.5
  52.6 22.5 %collective-permute-done.7 = bf16[192,1024]{1,0:T(8,128)(2,1)S(1)} collective-permute-done((bf16[192,1024]{1,0:T(8,128)(2,1)S(1)}, bf16[192,1024]{1,0:T(8,128)(2,1)S(1)}, u32[]{:S(2)}, u32[]{:S(2)}) %collective-permute-start.7) | collective-permute-done | bytes 393248 | tf_op jit(solution)/shard_map/ppermute | solution.py:149
  75.2 0.0 collective-permute-done.9
  75.2 1.1 %add_convert_fusion = bf16[192,1024]{1,0:T(8,128)(2,1)} fusion(bf16[192,1024]{1,0:T(8,128)(2,1)S(1)} %collective-permute-done.9, bf16[192,1024]{1,0:T(8,128)(2,1)S(1)} %collective-permute-done.7, bf16[192,1024]{1,0:T(8,128)(2,1)S(1)} %collective-permute-done.5, bf16[192,1024]{1,0:T(8,128)(2,1)S(1)} %collective-permute-done.3, ...), kind=kLoop, calls=%fused_computation | loop fusion | flops 2359296 | bytes 2359296 | tf_op jit(solution)/shard_map/convert_element_type | solution.py:205
Async XLA Ops:
  2.3 11.4 %collective-permute-start.2 = (bf16[1040,128]{1,0:T(8,128)(2,1)}, bf16[1040,128]{1,0:T(8,128)(2,1)S(1)}, u32[]{:S(2)}, u32[]{:S(2)}) collective-permute-start(bf16[1040,128]{1,0:T(8,128)(2,1)} %shard_map.103.refs_0_), channel_id=1, source_target_pairs={{0,24},{8,16},{16,8},{24,0},{1,25},{9,17},{17,9},{25,1},{2,26},{10... | collective-permute-start | bytes 798728 | tf_op jit(solution)/shard_map/ppermute | solution.py:146
  6.2 12.3 %collective-permute-start.1 = (bf16[1040,128]{1,0:T(8,128)(2,1)}, bf16[1040,128]{1,0:T(8,128)(2,1)S(1)}, u32[]{:S(2)}, u32[]{:S(2)}) collective-permute-start(bf16[1040,128]{1,0:T(8,128)(2,1)} %shard_map.103.refs_0_), channel_id=1, source_target_pairs={{0,16},{8,24},{16,0},{24,8},{1,17},{9,25},{17,1},{25,9},{2,18},{10... | collective-permute-start | bytes 798728 | tf_op jit(solution)/shard_map/ppermute | solution.py:146
  6.7 12.1 %collective-permute-start = (bf16[1040,128]{1,0:T(8,128)(2,1)}, bf16[1040,128]{1,0:T(8,128)(2,1)S(1)}, u32[]{:S(2)}, u32[]{:S(2)}) collective-permute-start(bf16[1040,128]{1,0:T(8,128)(2,1)} %shard_map.103.refs_0_), channel_id=1, source_target_pairs={{0,8},{8,0},{16,24},{24,16},{1,9},{9,1},{17,25},{25,17},{2,10},{10... | collective-permute-start | bytes 798728 | tf_op jit(solution)/shard_map/ppermute | solution.py:146
  18.8 1.0 %copy-start = (bf16[1040,128]{1,0:T(8,128)(2,1)S(1)}, bf16[1040,128]{1,0:T(8,128)(2,1)}, u32[]{:S(2)}) copy-start(bf16[1040,128]{1,0:T(8,128)(2,1)} %shard_map.103.refs_0_) | copy-start | bytes 798724
  30.6 5.7 %collective-permute-start.4 = (bf16[192,1024]{1,0:T(8,128)(2,1)S(1)}, bf16[192,1024]{1,0:T(8,128)(2,1)S(1)}, u32[]{:S(2)}, u32[]{:S(2)}) collective-permute-start(bf16[192,1024]{1,0:T(8,128)(2,1)S(1)} %get-tuple-element.22), channel_id=1, source_target_pairs={{0,1},{1,0},{2,3},{3,2},{4,5},{5,4},{6,7},{7,6},{8,9},{9,8},{10,11... | collective-permute-start | bytes 1179656 | tf_op jit(solution)/shard_map/ppermute | solution.py:149
  30.6 6.3 %collective-permute-start.6 = (bf16[192,1024]{1,0:T(8,128)(2,1)S(1)}, bf16[192,1024]{1,0:T(8,128)(2,1)S(1)}, u32[]{:S(2)}, u32[]{:S(2)}) collective-permute-start(bf16[192,1024]{1,0:T(8,128)(2,1)S(1)} %get-tuple-element.24), channel_id=1, source_target_pairs={{0,1},{1,0},{2,3},{3,2},{4,5},{5,4},{6,7},{7,6},{8,9},{9,8},{10,11... | collective-permute-start | bytes 1179656 | tf_op jit(solution)/shard_map/ppermute | solution.py:149
  31.1 21.1 %collective-permute-start.3 = (bf16[192,1024]{1,0:T(8,128)(2,1)S(1)}, bf16[192,1024]{1,0:T(8,128)(2,1)S(1)}, u32[]{:S(2)}, u32[]{:S(2)}) collective-permute-start(bf16[192,1024]{1,0:T(8,128)(2,1)S(1)} %get-tuple-element.20), channel_id=1, source_target_pairs={{0,1},{1,0},{2,3},{3,2},{4,5},{5,4},{6,7},{7,6},{8,9},{9,8},{10,11... | collective-permute-start | bytes 1179656 | tf_op jit(solution)/shard_map/ppermute | solution.py:149
  31.2 7.4 %collective-permute-start.8 = (bf16[192,1024]{1,0:T(8,128)(2,1)S(1)}, bf16[192,1024]{1,0:T(8,128)(2,1)S(1)}, u32[]{:S(2)}, u32[]{:S(2)}) collective-permute-start(bf16[192,1024]{1,0:T(8,128)(2,1)S(1)} %get-tuple-element.26), channel_id=1, source_target_pairs={{0,1},{1,0},{2,3},{3,2},{4,5},{5,4},{6,7},{7,6},{8,9},{9,8},{10,11... | collective-permute-start | bytes 1179656 | tf_op jit(solution)/shard_map/ppermute | solution.py:149
  31.7 1.1 %copy-start.1 = (bf16[16,192,128]{2,1,0:T(8,128)(2,1)S(1)}, bf16[16,192,128]{2,1,0:T(8,128)(2,1)}, u32[]{:S(2)}) copy-start(bf16[16,192,128]{2,1,0:T(8,128)(2,1)} %get-tuple-element.29.dps) | copy-start | bytes 2359300
  32.8 1.1 %copy-start.2 = (bf16[16,192,128]{2,1,0:T(8,128)(2,1)S(1)}, bf16[16,192,128]{2,1,0:T(8,128)(2,1)}, u32[]{:S(2)}) copy-start(bf16[16,192,128]{2,1,0:T(8,128)(2,1)} %get-tuple-element.30.hs) | copy-start | bytes 2359300
  34.7 9.2 %collective-permute-start.10 = (bf16[8,128,128]{2,1,0:T(8,128)(2,1)S(1)}, bf16[8,128,128]{2,1,0:T(8,128)(2,1)S(1)}, u32[]{:S(2)}, u32[]{:S(2)}) collective-permute-start(bf16[8,128,128]{2,1,0:T(8,128)(2,1)S(1)} %get-tuple-element.32), channel_id=1, source_target_pairs={{0,8},{8,0},{16,24},{24,16},{1,9},{9,1},{17,25},{25,17},{2,10},{10... | collective-permute-start | bytes 786440 | tf_op jit(solution)/shard_map/ppermute | solution.py:146
  36.3 13.6 %collective-permute-start.11 = (bf16[8,128,128]{2,1,0:T(8,128)(2,1)S(1)}, bf16[8,128,128]{2,1,0:T(8,128)(2,1)S(1)}, u32[]{:S(2)}, u32[]{:S(2)}) collective-permute-start(bf16[8,128,128]{2,1,0:T(8,128)(2,1)S(1)} %get-tuple-element.33), channel_id=1, source_target_pairs={{0,16},{8,24},{16,0},{24,8},{1,17},{9,25},{17,1},{25,9},{2,18},{10... | collective-permute-start | bytes 786440 | tf_op jit(solution)/shard_map/ppermute | solution.py:146
  36.9 14.5 %collective-permute-start.12 = (bf16[8,128,128]{2,1,0:T(8,128)(2,1)S(1)}, bf16[8,128,128]{2,1,0:T(8,128)(2,1)S(1)}, u32[]{:S(2)}, u32[]{:S(2)}) collective-permute-start(bf16[8,128,128]{2,1,0:T(8,128)(2,1)S(1)} %get-tuple-element.34), channel_id=1, source_target_pairs={{0,24},{8,16},{16,8},{24,0},{1,25},{9,17},{17,9},{25,1},{2,26},{10... | collective-permute-start | bytes 786440 | tf_op jit(solution)/shard_map/ppermute | solution.py:146
  38.6 14.0 %collective-permute-start.5 = (bf16[192,1024]{1,0:T(8,128)(2,1)S(1)}, bf16[192,1024]{1,0:T(8,128)(2,1)S(1)}, u32[]{:S(2)}, u32[]{:S(2)}) collective-permute-start(bf16[192,1024]{1,0:T(8,128)(2,1)S(1)} %add_convert_fusion.3), channel_id=1, source_target_pairs={{0,6},{1,7},{2,4},{3,5},{4,2},{5,3},{6,0},{7,1},{8,14},{9,15},{10,... | collective-permute-start | bytes 1179656 | tf_op jit(solution)/shard_map/ppermute | solution.py:149
  43.9 31.2 %collective-permute-start.7 = (bf16[192,1024]{1,0:T(8,128)(2,1)S(1)}, bf16[192,1024]{1,0:T(8,128)(2,1)S(1)}, u32[]{:S(2)}, u32[]{:S(2)}) collective-permute-start(bf16[192,1024]{1,0:T(8,128)(2,1)S(1)} %add_convert_fusion.2), channel_id=1, source_target_pairs={{0,4},{1,5},{2,6},{3,7},{4,0},{5,1},{6,2},{7,3},{8,12},{9,13},{10,... | collective-permute-start | bytes 1179656 | tf_op jit(solution)/shard_map/ppermute | solution.py:149
  49.9 25.3 %collective-permute-start.9 = (bf16[192,1024]{1,0:T(8,128)(2,1)S(1)}, bf16[192,1024]{1,0:T(8,128)(2,1)S(1)}, u32[]{:S(2)}, u32[]{:S(2)}) collective-permute-start(bf16[192,1024]{1,0:T(8,128)(2,1)S(1)} %add_convert_fusion.1), channel_id=1, source_target_pairs={{0,2},{1,3},{2,0},{3,1},{4,6},{5,7},{6,4},{7,5},{8,10},{9,11},{10,... | collective-permute-start | bytes 1179656 | tf_op jit(solution)/shard_map/ppermute | solution.py:149

commit v2 on v1

v2 whole, which is shorter than its diff:
```python
import functools

import jax
import jax.numpy as jnp
from jax import lax
from jax.experimental import pallas as pl
from jax.experimental.pallas import tpu as pltpu
from jax.sharding import PartitionSpec as P

FF = 32768
TILE = 128
IDX_ROWS = 16
BF16 = jnp.bfloat16
F32 = jnp.float32

VMEM = pl.BlockSpec(memory_space=pltpu.VMEM)
SMEM = pl.BlockSpec(memory_space=pltpu.SMEM)
ANY = pl.BlockSpec(memory_space=pl.ANY)
HBM = pl.BlockSpec(memory_space=pltpu.HBM)


def gelu_parts(pre):
    coef = 0.7978845608028654
    sq = pre * pre
    tanh_val = jnp.tanh(coef * (pre + 0.044715 * pre * sq))
    half = 0.5 * (1.0 + tanh_val)
    act = pre * half
    slope = half + 0.5 * pre * (1.0 - tanh_val * tanh_val) * coef * (
        1.0 + 3.0 * 0.044715 * sq
    )
    return (act, slope)


def pack(up_ref, places, out_ref):
    held = up_ref.shape[0]
    out_ref[: held * TILE] = up_ref[...].reshape(held * TILE, TILE)
    lane = lax.broadcasted_iota(jnp.int32, (IDX_ROWS, TILE), 1)
    val = jnp.zeros((IDX_ROWS, TILE), jnp.int32)
    for kind, ref in enumerate(places):
        for i in range(held):
            val = jnp.where(lane == kind * held + i, ref[0, i], val)
    out_ref[held * TILE :] = val.astype(F32).astype(BF16)


def pack_kernel(ur, uc, dr, dc, up, out):
    pack(up, (ur, uc, dr, dc), out)


def fetch_kernel(x, dy, x_out, dy_out, sem):
    copies = [
        pltpu.make_async_copy(x, x_out, sem.at[0]),
        pltpu.make_async_copy(dy, dy_out, sem.at[1]),
    ]
    for copy in copies:
        copy.start()
    for copy in copies:
        copy.wait()


def vmem_limit(mb):
    return pltpu.CompilerParams(vmem_limit_bytes=mb * 1024 * 1024)


def dot(a, b, dims):
    return lax.dot_general(a, b, (dims, ((), ())), preferred_element_type=F32)


def main_kernel(n_f, held, n_z, per_dev, z_ref, x_ref, dy_ref, *refs):
    ups, downs = refs[:n_f], refs[n_f : 2 * n_f]
    refs = refs[2 * n_f :]
    mine, other = refs[:n_z], refs[n_z : 2 * n_z]
    xs, dys, dps, hs = refs[2 * n_z : 2 * n_z + 4]
    (prod, back, rprod, hid, dpre, out, idx_v, idx, first, d_first, r_first, lead, sem_i) = refs[
        2 * n_z + 4 :
    ]
    slots = n_f * held
    z, core = z_ref[0], z_ref[1]
    for f in range(n_f):
        idx_v[f : f + 1] = ups[f][held * TILE :][:1].astype(F32).astype(jnp.int32)
    copy = pltpu.make_async_copy(idx_v, idx, sem_i)
    copy.start()
    copy.wait()

    def at(kind, s):
        return idx[s // held, kind * held + s % held]

    def block(ref, which):
        return ref[:, pl.ds(pl.multiple_of(which * TILE, TILE), TILE)]

    out[...] = jnp.zeros_like(out)
    back[slots] = jnp.zeros_like(back[slots])
    hid[slots] = jnp.zeros_like(hid[slots])
    for table, kind in ((first, 1), (d_first, 2), (r_first, 0)):
        for c in range(table.shape[0]):
            table[c] = -1
        for s in range(slots):
            c = at(kind, s)
            seen = table[c]
            leader = jnp.where(seen < 0, s, seen)
            table[c] = leader
            lead[kind, s] = leader

    def up_tile(s):
        return ups[s // held][pl.ds((s % held) * TILE, TILE)]

    def down_tile(s):
        return downs[s // held][s % held]

    def fold(buf, kind):
        for s in range(1, slots):
            leader = lead[kind, s]

            @pl.when(leader != s)
            def _():
                buf[leader] += buf[s]

    for s in range(slots):
        x = block(x_ref, at(0, s))
        xs[s] = x
        prod[s] = dot(x, up_tile(s), ((1,), (0,)))
    for s in range(slots):
        dy = block(dy_ref, at(3, s))
        dys[s] = dy
        back[s] = dot(dy, down_tile(s), ((1,), (1,)))
    fold(prod, 1)
    fold(back, 2)
    for s in range(slots):

        @pl.when(lead[1, s] == s)
        def _():
            act, slope = gelu_parts(prod[s])
            d = d_first[at(1, s)]
            hid[s] = act.astype(BF16)
            dpre[s] = (back[jnp.where(d < 0, slots, d)] * slope).astype(BF16)

    for s in range(slots):
        dp = dpre[lead[1, s]]
        dps[s] = dp
        rprod[s] = dot(dp, up_tile(s), ((1,), (1,)))
        h = first[at(2, s)]
        hs[s] = hid[jnp.where(h < 0, slots, h)]
    fold(rprod, 0)
    for s in range(slots):

        @pl.when(lead[0, s] == s)
        def _():
            r = at(0, s)
            dev, j = r // per_dev, r % per_dev
            to_z, to_core = dev // 2, dev % 2
            k = n_z - 1 - jnp.bitwise_xor(to_z, z) if n_z == 4 else to_z
            whose = jnp.bitwise_xor(to_core, core)
            col = pl.ds(pl.multiple_of(j * TILE, TILE), TILE)
            out[whose * n_z + k, :, col] = rprod[s].astype(BF16)

    for k in range(n_z):
        mine[k][...] = out[k]
        other[k][...] = out[n_z + k]


def add_kernel(a, b, out):
    out[...] = a[...].astype(F32) + b[...].astype(F32)


def main_call(n_f, held, n_z, per_dev, group_cols, place, inputs, cotangent, tiles):
    tok, width = inputs.shape
    slots = n_f * held
    shard = jax.ShapeDtypeStruct((tok, per_dev * TILE), BF16)
    sel = jax.ShapeDtypeStruct((slots, tok, TILE), BF16)
    return pl.pallas_call(
        functools.partial(main_kernel, n_f, held, n_z, per_dev),
        out_shape=[shard] * (2 * n_z) + [sel] * 4,
        in_specs=[SMEM] + [VMEM] * (2 + 2 * n_f),
        out_specs=[VMEM] * (2 * n_z + 4),
        scratch_shapes=[
            pltpu.VMEM((slots, tok, TILE), F32),
            pltpu.VMEM((slots + 1, tok, TILE), F32),
            pltpu.VMEM((slots, tok, TILE), F32),
            pltpu.VMEM((slots + 1, tok, TILE), BF16),
            pltpu.VMEM((slots, tok, TILE), BF16),
            pltpu.VMEM((2 * n_z, tok, per_dev * TILE), BF16),
            pltpu.VMEM((n_f, TILE), jnp.int32),
            pltpu.SMEM((n_f, TILE), jnp.int32),
            pltpu.SMEM((group_cols,), jnp.int32),
            pltpu.SMEM((group_cols,), jnp.int32),
            pltpu.SMEM((width // TILE,), jnp.int32),
            pltpu.SMEM((3, slots), jnp.int32),
            pltpu.SemaphoreType.DMA,
        ],
        compiler_params=vmem_limit(24 if slots <= 16 else 56),
    )(place, inputs, cotangent, *tiles)


def grad_kernel(n_f, held, after, xs, dys, dps, hs, *outs):
    for s in range(n_f * held):
        f, i = s // held, s % held
        outs[f][i] = dot(xs[s], dps[s], ((0,), (0,))).astype(BF16)
        outs[f][held + i] = dot(hs[s], dys[s], ((0,), (0,))).astype(BF16)


def on_device(inputs, cotangent, up_tiles, up_rows, up_cols, down_tiles, down_rows, down_cols):
    n_f, n_t = lax.axis_size("fsdp"), lax.axis_size("tensor")
    n_z = n_t // 2
    tok, width = inputs.shape
    per_dev = width // (n_t * TILE)
    group_cols = FF // (n_t * TILE)
    held = up_tiles.shape[1]
    rows = held * TILE
    slots = held * n_f
    t = lax.axis_index("tensor")
    z, core = t // 2, t % 2

    zc = jnp.stack([z, core]).astype(jnp.int32)

    def over_f(a, k):
        return lax.ppermute(a, "fsdp", [(f, f ^ k) for f in range(n_f)])

    def over_t(a, k):
        return lax.ppermute(a, "tensor", [(i, i ^ k) for i in range(n_t)])

    up, down = up_tiles[0], down_tiles[0]
    where = (up_rows, up_cols, down_rows, down_cols)
    packed = jax.ShapeDtypeStruct((held * TILE + IDX_ROWS, TILE), BF16)
    downs = [over_f(down, k) for k in range(1, n_f)]
    sent = pl.pallas_call(
        pack_kernel,
        out_shape=packed,
        in_specs=[SMEM] * 4 + [VMEM],
        out_specs=VMEM,
    )(*where, up)
    x_v, dy_v = pl.pallas_call(
        fetch_kernel,
        out_shape=[jax.ShapeDtypeStruct(inputs.shape, BF16)] * 2,
        in_specs=[HBM, HBM],
        out_specs=[VMEM, VMEM],
        scratch_shapes=[pltpu.SemaphoreType.DMA((2,))],
        compiler_params=vmem_limit(16),
    )(inputs, cotangent)
    ups = [over_f(sent, k) for k in range(1, n_f)]
    tiles = [sent] + ups + [down] + downs
    outs = main_call(
        n_f, held, n_z, per_dev, group_cols, zc, x_v, dy_v, tiles
    )
    mine, other = outs[:n_z], outs[n_z : 2 * n_z]
    chosen = outs[2 * n_z :]
    parts = [
        (m.astype(F32) + over_t(o, 1).astype(F32)).astype(BF16)
        for m, o in zip(mine, other)
    ]
    if n_z == 4:
        far, cross, near, own = parts
        passed = over_t(far, 2)
        came = over_t(near, 2)
        across = over_t((cross.astype(F32) + passed.astype(F32)).astype(BF16), 4)
        acc = pl.pallas_call(
            add_kernel,
            out_shape=jax.ShapeDtypeStruct(own.shape, F32),
            in_specs=[VMEM] * 2,
            out_specs=VMEM,
            compiler_params=vmem_limit(8),
        )(own, came)
        input_grad = (acc + across.astype(F32)).astype(BF16)
        gate = near
    else:
        input_grad = lax.psum_scatter(
            jnp.stack(parts),
            "tensor",
            scatter_dimension=0,
            tiled=False,
            axis_index_groups=[list(range(c, n_t, 2)) for c in range(2)],
        )
        gate = parts[0]
    terms = pl.pallas_call(
        functools.partial(grad_kernel, n_f, held),
        out_shape=[jax.ShapeDtypeStruct((2 * held, TILE, TILE), BF16)] * n_f,
        in_specs=[ANY] + [VMEM] * 4,
        out_specs=[VMEM] * n_f,
        compiler_params=vmem_limit(16),
    )(gate, *chosen)
    total = terms[0].astype(F32)
    for k in range(1, n_f):
        total = total + over_f(terms[k], k).astype(F32)
    total = total.astype(BF16)
    return (input_grad, total[:held][None], total[held:][None])


def solution(mesh):
    placed = (
        P("fsdp", None),
        P("fsdp", None),
        P("tensor", "fsdp", None, None),
        P("tensor", "fsdp"),
        P("tensor", "fsdp"),
        P("tensor", "fsdp", None, None),
        P("tensor", "fsdp"),
        P("tensor", "fsdp"),
    )
    return jax.shard_map(
        on_device,
        mesh=mesh,
        in_specs=placed,
        out_specs=(
            P("fsdp", "tensor"),
            P("tensor", "fsdp", None, None),
            P("tensor", "fsdp", None, None),
        ),
        check_vma=False,
    )
```

time: 76.6 us -> 56.2 us (0.73)
  waiting for transfers between devices: 39.9 us -> 23.9 us
  Pallas kernels: 13.2 us -> 7.62 us
    ppermute x6 -> x9, waiting for transfers between devices: 17 us -> 5.59 us  [over_f(): return lax.ppermute(a, 'fsdp', [(f, f ^ k) for f in range(n_f)])]
    pallas_call x2 -> x4, Pallas kernels: 12.5 us -> 6.86 us  [the longest x1 4.75 us: main_call(): pl.pallas_call(functools.partial(main_kernel, n_f, held, n_z, per_dev), o...]
    ppermute x7, waiting for transfers between devices: 22.9 us -> 18.3 us  [over_t(): return lax.ppermute(a, 'tensor', [(i, i ^ k) for i in range(n_t)])]
    ppermute x6 -> x9, starting transfers between devices: 8.08 us -> 11.6 us  [over_f(): return lax.ppermute(a, 'fsdp', [(f, f ^ k) for f in range(n_f)])]
    ppermute x7, starting transfers between devices: 8.72 us -> 5.86 us  [over_t(): return lax.ppermute(a, 'tensor', [(i, i ^ k) for i in range(n_t)])]
    unnamed x6 -> x8, local copies, waits for them, and re-layouts: 3.22 us -> 3.79 us
  transfers between devices with their start and end apart: 13 -> 16, of which waited for: 7 -> 6; matrix products, arithmetic and copies ran while one was open for 2% -> 3% of each run, Pallas kernels for 1% -> 5%
where the time goes in v2:
time: 56.2 us; the launch traced here: 55.9 us
  waiting for transfers between devices  23.9 us (43%)
  starting transfers between devices  17.5 us (31%)
  Pallas kernels  7.62 us (14%)
  local copies, waits for them, and re-layouts  4.5 us (8%)
  other arithmetic  1.65 us (3%)
  between operations  0.75 us (1%)
    ppermute x7, waiting for transfers between devices, over_t(): return lax.ppermute(a, 'tensor', [(i, i ^ k) for i in range(n_t)])  18.3 us
    ppermute x9, starting transfers between devices, over_f(): return lax.ppermute(a, 'fsdp', [(f, f ^ k) for f in range(n_f)])  11.6 us
    ppermute x7, starting transfers between devices, over_t(): return lax.ppermute(a, 'tensor', [(i, i ^ k) for i in range(n_t)])  5.86 us
    ppermute x9, waiting for transfers between devices, over_f(): return lax.ppermute(a, 'fsdp', [(f, f ^ k) for f in range(n_f)])  5.59 us
    pallas_call x1, Pallas kernels, main_call(): pl.pallas_call(functools.partial(main_kernel, n_f, held, n_z, per_dev), o...  4.75 us
    unnamed x8, local copies, waits for them, and re-layouts  3.79 us
    pallas_call x1, Pallas kernels, on_device(): pl.pallas_call(pack_kernel, out_shape=packed, in_specs=[SMEM] * 4 + [VMEM...  1.59 us
  transfers between devices with their start and end apart: 16, of which 6 were waited for; matrix products, arithmetic and copies ran while one was open for 3% of the time, Pallas kernels for 5%

profile of v2, /device:TPU:0, one launch (start us, length us, event | category | flops | bytes accessed | tf_op | source)
XLA Modules:
  0.0 55.9 jit_solution(11264343834469368617)
XLA Ops:
  0.6 4.0 %collective-permute-start.5 = (bf16[4,128,128]{2,1,0:T(8,128)(2,1)}, bf16[4,128,128]{2,1,0:T(8,128)(2,1)S(1)}, u32[]{:S(2)}, u32[]{:S(2)}) collective-permute-start(bf16[4,128,128]{2,1,0:T(8,128)(2,1)} %bitcast.8), channel_id=1, source_target_pairs={{0,24},{8,16},{16,8},{24,0},{1,25},{9,17},{17,9},{25,1},{2,26},{10... | collective-permute-start | bytes 393224 | tf_op jit(solution)/shard_map/ppermute | solution.py:215
  4.6 1.6 %shard_map.104.refs_0_ = bf16[528,128]{1,0:T(8,128)(2,1)} custom-call(s32[1,4]{1,0:T(1,128)} %ur.1, s32[1,4]{1,0:T(1,128)} %uc.1, s32[1,4]{1,0:T(1,128)} %dr.1, s32[1,4]{1,0:T(1,128)} %dc.1, bf16[4,128,128]{2,1,0:T(8,128)(2,1)} %bitcast.12), custom_call_target="tpu_custom_call" | custom-call | tf_op jit(solution)/shard_map/pallas_call | solution.py:224
  6.2 0.0 collective-permute-start.2
  6.2 2.0 %collective-permute-start.1 = (bf16[528,128]{1,0:T(8,128)(2,1)}, bf16[528,128]{1,0:T(8,128)(2,1)S(1)}, u32[]{:S(2)}, u32[]{:S(2)}) collective-permute-start(bf16[528,128]{1,0:T(8,128)(2,1)} %shard_map.104.refs_0_), channel_id=1, source_target_pairs={{0,16},{8,24},{16,0},{24,8},{1,17},{9,25},{17,1},{25,9},{2,18},{10... | collective-permute-start | bytes 405512 | tf_op jit(solution)/shard_map/ppermute | solution.py:215
  8.2 1.5 %collective-permute-start = (bf16[528,128]{1,0:T(8,128)(2,1)}, bf16[528,128]{1,0:T(8,128)(2,1)S(1)}, u32[]{:S(2)}, u32[]{:S(2)}) collective-permute-start(bf16[528,128]{1,0:T(8,128)(2,1)} %shard_map.104.refs_0_), channel_id=1, source_target_pairs={{0,8},{8,0},{16,24},{24,16},{1,9},{9,1},{17,25},{25,17},{2,10},{10... | collective-permute-start | bytes 405512 | tf_op jit(solution)/shard_map/ppermute | solution.py:215
  9.7 0.5 collective-permute-start.4
  10.2 0.0 collective-permute-done.5.refs_7_
  10.2 0.1 collective-permute-start.3
  10.3 0.0 copy-start
  10.3 1.9 %copy-done = bf16[192,8192]{1,0:T(8,128)(2,1)S(1)} copy-done((bf16[192,8192]{1,0:T(8,128)(2,1)S(1)}, bf16[192,8192]{1,0:T(8,128)(2,1)}, u32[]{:S(2)}) %copy-start) | copy-done | bytes 3145752
  12.1 0.0 copy-start.1
  12.1 1.9 %copy-done.1 = bf16[192,8192]{1,0:T(8,128)(2,1)S(1)} copy-done((bf16[192,8192]{1,0:T(8,128)(2,1)S(1)}, bf16[192,8192]{1,0:T(8,128)(2,1)}, u32[]{:S(2)}) %copy-start.1) | copy-done | bytes 3145752
  14.0 0.0 copy-start.2
  14.0 0.0 copy-start.3
  14.0 0.4 shard_map.103
  14.5 0.1 pad_add_fusion.z_ref
  14.6 2.6 %collective-permute-done.4.refs_6_ = bf16[4,128,128]{2,1,0:T(8,128)(2,1)S(1)} collective-permute-done((bf16[4,128,128]{2,1,0:T(8,128)(2,1)}, bf16[4,128,128]{2,1,0:T(8,128)(2,1)S(1)}, u32[]{:S(2)}, u32[]{:S(2)}) %collective-permute-start.4) | collective-permute-done | bytes 131104 | tf_op jit(solution)/shard_map/ppermute | solution.py:215
  17.2 0.0 collective-permute-done.3.refs_5_
  17.2 0.0 collective-permute-done.2.refs_3_
  17.2 0.0 collective-permute-done.1.refs_2_
  17.2 0.0 collective-permute-done.refs_1_
  17.2 0.0 copy-done.2
  17.2 0.0 copy-done.3
  17.2 4.8 %shard_map.105 = (bf16[192,1024]{1,0:T(8,128)(2,1)S(1)}, bf16[192,1024]{1,0:T(8,128)(2,1)S(1)}, bf16[192,1024]{1,0:T(8,128)(2,1)S(1)}, bf16[192,1024]{1,0:T(8,12...) custom-call(s32[2]{0:T(128)S(1)} %pad_add_fusion.z_ref, ...), custom_call_target="tpu_custom_call" | custom-call | tf_op jit(solution)/shard_map/pallas_call | solution.py:169
  22.0 0.1 collective-permute-start.10
  22.1 0.5 collective-permute-start.7
  22.6 0.1 collective-permute-start.6
  22.6 0.4 collective-permute-start.9
  23.1 0.7 %collective-permute-done.10 = bf16[192,1024]{1,0:T(8,128)(2,1)S(1)} collective-permute-done((bf16[192,1024]{1,0:T(8,128)(2,1)S(1)}, bf16[192,1024]{1,0:T(8,128)(2,1)S(1)}, u32[]{:S(2)}, u32[]{:S(2)}) %collective-permute-start.10) | collective-permute-done | bytes 393248 | tf_op jit(solution)/shard_map/ppermute | solution.py:218
  23.8 0.1 add_convert_fusion.2
  23.9 1.7 %collective-permute-start.11 = (bf16[192,1024]{1,0:T(8,128)(2,1)S(1)}, bf16[192,1024]{1,0:T(8,128)(2,1)S(1)}, u32[]{:S(2)}, u32[]{:S(2)}) collective-permute-start(bf16[192,1024]{1,0:T(8,128)(2,1)S(1)} %add_convert_fusion.2), channel_id=1, source_target_pairs={{0,2},{1,3},{2,0},{3,1},{4,6},{5,7},{6,4},{7,5},{8,10},{9,11},{10,... | collective-permute-start | bytes 1179656 | tf_op jit(solution)/shard_map/ppermute | solution.py:218
  25.6 0.0 collective-permute-done.7
  25.6 0.1 add_convert_fusion.4.after
  25.7 0.5 collective-permute-start.8
  26.2 0.8 %shard_map.107 = (bf16[8,128,128]{2,1,0:T(8,128)(2,1)S(1)}, bf16[8,128,128]{2,1,0:T(8,128)(2,1)S(1)}, bf16[8,128,128]{2,1,0:T(8,128)(2,1)S(1)}, bf16[8,128,128]{2,1,0:T(8,128)(2,1)S(1)}) custom-call(bf16[192,1024]{1,0:T(8,128)(2,1)S(1)} %add_convert_fusion.4.after, bf16[16,192,128]{2,1,0:T(8,128)(2,1)S(1)} %get-tuple-element.31.xs, ...), custom_call_target="tpu_custom_call" | custom-call | tf_op jit(solution)/shard_map/pallas_call | solution.py:272
  27.0 1.5 %collective-permute-start.13 = (bf16[8,128,128]{2,1,0:T(8,128)(2,1)S(1)}, bf16[8,128,128]{2,1,0:T(8,128)(2,1)S(1)}, u32[]{:S(2)}, u32[]{:S(2)}) collective-permute-start(bf16[8,128,128]{2,1,0:T(8,128)(2,1)S(1)} %get-tuple-element.36), channel_id=1, source_target_pairs={{0,8},{8,0},{16,24},{24,16},{1,9},{9,1},{17,25},{25,17},{2,10},{10... | collective-permute-start | bytes 786440 | tf_op jit(solution)/shard_map/ppermute | solution.py:215
  28.5 0.0 collective-permute-done.6
  28.5 1.5 %collective-permute-start.14 = (bf16[8,128,128]{2,1,0:T(8,128)(2,1)S(1)}, bf16[8,128,128]{2,1,0:T(8,128)(2,1)S(1)}, u32[]{:S(2)}, u32[]{:S(2)}) collective-permute-start(bf16[8,128,128]{2,1,0:T(8,128)(2,1)S(1)} %get-tuple-element.37), channel_id=1, source_target_pairs={{0,16},{8,24},{16,0},{24,8},{1,17},{9,25},{17,1},{25,9},{2,18},{10... | collective-permute-start | bytes 786440 | tf_op jit(solution)/shard_map/ppermute | solution.py:215
  30.0 0.1 add_convert_fusion.5.a
  30.1 0.0 collective-permute-done.9
  30.1 0.6 %collective-permute-start.15 = (bf16[8,128,128]{2,1,0:T(8,128)(2,1)S(1)}, bf16[8,128,128]{2,1,0:T(8,128)(2,1)S(1)}, u32[]{:S(2)}, u32[]{:S(2)}) collective-permute-start(bf16[8,128,128]{2,1,0:T(8,128)(2,1)S(1)} %get-tuple-element.38), channel_id=1, source_target_pairs={{0,24},{8,16},{16,8},{24,0},{1,25},{9,17},{17,9},{25,1},{2,26},{10... | collective-permute-start | bytes 786440 | tf_op jit(solution)/shard_map/ppermute | solution.py:215
  30.8 5.2 %collective-permute-done.11 = bf16[192,1024]{1,0:T(8,128)(2,1)S(1)} collective-permute-done((bf16[192,1024]{1,0:T(8,128)(2,1)S(1)}, bf16[192,1024]{1,0:T(8,128)(2,1)S(1)}, u32[]{:S(2)}, u32[]{:S(2)}) %collective-permute-start.11) | collective-permute-done | bytes 393248 | tf_op jit(solution)/shard_map/ppermute | solution.py:218
  35.9 0.2 add_convert_fusion.1
  36.1 2.6 %collective-permute-start.12 = (bf16[192,1024]{1,0:T(8,128)(2,1)S(1)}, bf16[192,1024]{1,0:T(8,128)(2,1)S(1)}, u32[]{:S(2)}, u32[]{:S(2)}) collective-permute-start(bf16[192,1024]{1,0:T(8,128)(2,1)S(1)} %add_convert_fusion.1), channel_id=1, source_target_pairs={{0,4},{1,5},{2,6},{3,7},{4,0},{5,1},{6,2},{7,3},{8,12},{9,13},{10,... | collective-permute-start | bytes 1179656 | tf_op jit(solution)/shard_map/ppermute | solution.py:218
  38.8 0.0 collective-permute-done.13
  38.8 3.0 %collective-permute-done.14 = bf16[8,128,128]{2,1,0:T(8,128)(2,1)S(1)} collective-permute-done((bf16[8,128,128]{2,1,0:T(8,128)(2,1)S(1)}, bf16[8,128,128]{2,1,0:T(8,128)(2,1)S(1)}, u32[]{:S(2)}, u32[]{:S(2)}) %collective-permute-start.14) | collective-permute-done | bytes 262176 | tf_op jit(solution)/shard_map/ppermute | solution.py:215
  41.7 0.0 collective-permute-done.15
  41.7 0.1 add_convert_fusion.6
  41.9 0.7 %slice_bitcast_fusion = (bf16[1,4,128,128]{3,2,1,0:T(8,128)(2,1)}, bf16[1,4,128,128]{3,2,1,0:T(8,128)(2,1)}) fusion(bf16[8,128,128]{2,1,0:T(8,128)(2,1)S(1)} %add_convert_fusion.6), kind=kLoop, calls=%fused_computation.7 | loop fusion | bytes 524288 | tf_op jit(solution)/shard_map/broadcast_in_dim | solution.py:283
  42.6 8.4 %collective-permute-done.8.b = bf16[192,1024]{1,0:T(8,128)(2,1)S(1)} collective-permute-done((bf16[192,1024]{1,0:T(8,128)(2,1)S(1)}, bf16[192,1024]{1,0:T(8,128)(2,1)S(1)}, u32[]{:S(2)}, u32[]{:S(2)}) %collective-permute-start.8) | collective-permute-done | bytes 393248 | tf_op jit(solution)/shard_map/ppermute | solution.py:218
  51.0 0.1 shard_map.106
  51.1 4.1 %collective-permute-done.12 = bf16[192,1024]{1,0:T(8,128)(2,1)S(1)} collective-permute-done((bf16[192,1024]{1,0:T(8,128)(2,1)S(1)}, bf16[192,1024]{1,0:T(8,128)(2,1)S(1)}, u32[]{:S(2)}, u32[]{:S(2)}) %collective-permute-start.12) | collective-permute-done | bytes 393248 | tf_op jit(solution)/shard_map/ppermute | solution.py:218
  55.1 0.8 %add_convert_fusion = bf16[192,1024]{1,0:T(8,128)(2,1)} fusion(f32[192,1024]{1,0:T(8,128)S(1)} %shard_map.106, bf16[192,1024]{1,0:T(8,128)(2,1)S(1)} %collective-permute-done.12), kind=kLoop, calls=%fused_computation | loop fusion | flops 589824 | bytes 1572864 | tf_op jit(solution)/shard_map/convert_element_type | solution.py:261
Async XLA Ops:
  0.6 9.5 %collective-permute-start.5 = (bf16[4,128,128]{2,1,0:T(8,128)(2,1)}, bf16[4,128,128]{2,1,0:T(8,128)(2,1)S(1)}, u32[]{:S(2)}, u32[]{:S(2)}) collective-permute-start(bf16[4,128,128]{2,1,0:T(8,128)(2,1)} %bitcast.8), channel_id=1, source_target_pairs={{0,24},{8,16},{16,8},{24,0},{1,25},{9,17},{17,9},{25,1},{2,26},{10... | collective-permute-start | bytes 393224 | tf_op jit(solution)/shard_map/ppermute | solution.py:215
  6.2 11.0 %collective-permute-start.2 = (bf16[528,128]{1,0:T(8,128)(2,1)}, bf16[528,128]{1,0:T(8,128)(2,1)S(1)}, u32[]{:S(2)}, u32[]{:S(2)}) collective-permute-start(bf16[528,128]{1,0:T(8,128)(2,1)} %shard_map.104.refs_0_), channel_id=1, source_target_pairs={{0,24},{8,16},{16,8},{24,0},{1,25},{9,17},{17,9},{25,1},{2,26},{10... | collective-permute-start | bytes 405512 | tf_op jit(solution)/shard_map/ppermute | solution.py:215
  6.2 11.0 %collective-permute-start.1 = (bf16[528,128]{1,0:T(8,128)(2,1)}, bf16[528,128]{1,0:T(8,128)(2,1)S(1)}, u32[]{:S(2)}, u32[]{:S(2)}) collective-permute-start(bf16[528,128]{1,0:T(8,128)(2,1)} %shard_map.104.refs_0_), channel_id=1, source_target_pairs={{0,16},{8,24},{16,0},{24,8},{1,17},{9,25},{17,1},{25,9},{2,18},{10... | collective-permute-start | bytes 405512 | tf_op jit(solution)/shard_map/ppermute | solution.py:215
  8.2 9.0 %collective-permute-start = (bf16[528,128]{1,0:T(8,128)(2,1)}, bf16[528,128]{1,0:T(8,128)(2,1)S(1)}, u32[]{:S(2)}, u32[]{:S(2)}) collective-permute-start(bf16[528,128]{1,0:T(8,128)(2,1)} %shard_map.104.refs_0_), channel_id=1, source_target_pairs={{0,8},{8,0},{16,24},{24,16},{1,9},{9,1},{17,25},{25,17},{2,10},{10... | collective-permute-start | bytes 405512 | tf_op jit(solution)/shard_map/ppermute | solution.py:215
  9.7 7.5 %collective-permute-start.4 = (bf16[4,128,128]{2,1,0:T(8,128)(2,1)}, bf16[4,128,128]{2,1,0:T(8,128)(2,1)S(1)}, u32[]{:S(2)}, u32[]{:S(2)}) collective-permute-start(bf16[4,128,128]{2,1,0:T(8,128)(2,1)} %bitcast.9), channel_id=1, source_target_pairs={{0,16},{8,24},{16,0},{24,8},{1,17},{9,25},{17,1},{25,9},{2,18},{10... | collective-permute-start | bytes 393224 | tf_op jit(solution)/shard_map/ppermute | solution.py:215
  10.2 7.0 %collective-permute-start.3 = (bf16[4,128,128]{2,1,0:T(8,128)(2,1)}, bf16[4,128,128]{2,1,0:T(8,128)(2,1)S(1)}, u32[]{:S(2)}, u32[]{:S(2)}) collective-permute-start(bf16[4,128,128]{2,1,0:T(8,128)(2,1)} %bitcast.10), channel_id=1, source_target_pairs={{0,8},{8,0},{16,24},{24,16},{1,9},{9,1},{17,25},{25,17},{2,10},{10... | collective-permute-start | bytes 393224 | tf_op jit(solution)/shard_map/ppermute | solution.py:215
  10.3 1.9 %copy-start = (bf16[192,8192]{1,0:T(8,128)(2,1)S(1)}, bf16[192,8192]{1,0:T(8,128)(2,1)}, u32[]{:S(2)}) copy-start(bf16[192,8192]{1,0:T(8,128)(2,1)} %x.1) | copy-start | bytes 9437188
  12.1 1.9 %copy-start.1 = (bf16[192,8192]{1,0:T(8,128)(2,1)S(1)}, bf16[192,8192]{1,0:T(8,128)(2,1)}, u32[]{:S(2)}) copy-start(bf16[192,8192]{1,0:T(8,128)(2,1)} %dy.1) | copy-start | bytes 9437188
  14.0 3.2 %copy-start.2 = (bf16[528,128]{1,0:T(8,128)(2,1)S(1)}, bf16[528,128]{1,0:T(8,128)(2,1)}, u32[]{:S(2)}) copy-start(bf16[528,128]{1,0:T(8,128)(2,1)} %shard_map.104.refs_0_) | copy-start | bytes 405508
  14.0 3.2 %copy-start.3 = (bf16[1,4,128,128]{3,2,1,0:T(8,128)(2,1)S(1)}, bf16[1,4,128,128]{3,2,1,0:T(8,128)(2,1)}, u32[]{:S(2)}) copy-start(bf16[1,4,128,128]{3,2,1,0:T(8,128)(2,1)} %param.13) | copy-start | bytes 393220
  22.0 1.8 %collective-permute-start.10 = (bf16[192,1024]{1,0:T(8,128)(2,1)S(1)}, bf16[192,1024]{1,0:T(8,128)(2,1)S(1)}, u32[]{:S(2)}, u32[]{:S(2)}) collective-permute-start(bf16[192,1024]{1,0:T(8,128)(2,1)S(1)} %get-tuple-element.30), channel_id=1, source_target_pairs={{0,1},{1,0},{2,3},{3,2},{4,5},{5,4},{6,7},{7,6},{8,9},{9,8},{10,11... | collective-permute-start | bytes 1179656 | tf_op jit(solution)/shard_map/ppermute | solution.py:218
  22.1 3.5 %collective-permute-start.7 = (bf16[192,1024]{1,0:T(8,128)(2,1)S(1)}, bf16[192,1024]{1,0:T(8,128)(2,1)S(1)}, u32[]{:S(2)}, u32[]{:S(2)}) collective-permute-start(bf16[192,1024]{1,0:T(8,128)(2,1)S(1)} %get-tuple-element.26), channel_id=1, source_target_pairs={{0,1},{1,0},{2,3},{3,2},{4,5},{5,4},{6,7},{7,6},{8,9},{9,8},{10,11... | collective-permute-start | bytes 1179656 | tf_op jit(solution)/shard_map/ppermute | solution.py:218
  22.6 5.9 %collective-permute-start.6 = (bf16[192,1024]{1,0:T(8,128)(2,1)S(1)}, bf16[192,1024]{1,0:T(8,128)(2,1)S(1)}, u32[]{:S(2)}, u32[]{:S(2)}) collective-permute-start(bf16[192,1024]{1,0:T(8,128)(2,1)S(1)} %get-tuple-element.24), channel_id=1, source_target_pairs={{0,1},{1,0},{2,3},{3,2},{4,5},{5,4},{6,7},{7,6},{8,9},{9,8},{10,11... | collective-permute-start | bytes 1179656 | tf_op jit(solution)/shard_map/ppermute | solution.py:218
  22.6 7.5 %collective-permute-start.9 = (bf16[192,1024]{1,0:T(8,128)(2,1)S(1)}, bf16[192,1024]{1,0:T(8,128)(2,1)S(1)}, u32[]{:S(2)}, u32[]{:S(2)}) collective-permute-start(bf16[192,1024]{1,0:T(8,128)(2,1)S(1)} %get-tuple-element.28), channel_id=1, source_target_pairs={{0,1},{1,0},{2,3},{3,2},{4,5},{5,4},{6,7},{7,6},{8,9},{9,8},{10,11... | collective-permute-start | bytes 1179656 | tf_op jit(solution)/shard_map/ppermute | solution.py:218
  23.9 12.0 %collective-permute-start.11 = (bf16[192,1024]{1,0:T(8,128)(2,1)S(1)}, bf16[192,1024]{1,0:T(8,128)(2,1)S(1)}, u32[]{:S(2)}, u32[]{:S(2)}) collective-permute-start(bf16[192,1024]{1,0:T(8,128)(2,1)S(1)} %add_convert_fusion.2), channel_id=1, source_target_pairs={{0,2},{1,3},{2,0},{3,1},{4,6},{5,7},{6,4},{7,5},{8,10},{9,11},{10,... | collective-permute-start | bytes 1179656 | tf_op jit(solution)/shard_map/ppermute | solution.py:218
  25.7 25.2 %collective-permute-start.8 = (bf16[192,1024]{1,0:T(8,128)(2,1)S(1)}, bf16[192,1024]{1,0:T(8,128)(2,1)S(1)}, u32[]{:S(2)}, u32[]{:S(2)}) collective-permute-start(bf16[192,1024]{1,0:T(8,128)(2,1)S(1)} %add_convert_fusion.4.after), channel_id=1, source_target_pairs={{0,2},{1,3},{2,0},{3,1},{4,6},{5,7},{6,4},{7,5},{8,10},{9,11},{10,... | collective-permute-start | bytes 1179656 | tf_op jit(solution)/shard_map/ppermute | solution.py:218
  27.0 11.8 %collective-permute-start.13 = (bf16[8,128,128]{2,1,0:T(8,128)(2,1)S(1)}, bf16[8,128,128]{2,1,0:T(8,128)(2,1)S(1)}, u32[]{:S(2)}, u32[]{:S(2)}) collective-permute-start(bf16[8,128,128]{2,1,0:T(8,128)(2,1)S(1)} %get-tuple-element.36), channel_id=1, source_target_pairs={{0,8},{8,0},{16,24},{24,16},{1,9},{9,1},{17,25},{25,17},{2,10},{10... | collective-permute-start | bytes 786440 | tf_op jit(solution)/shard_map/ppermute | solution.py:215
  28.5 13.2 %collective-permute-start.14 = (bf16[8,128,128]{2,1,0:T(8,128)(2,1)S(1)}, bf16[8,128,128]{2,1,0:T(8,128)(2,1)S(1)}, u32[]{:S(2)}, u32[]{:S(2)}) collective-permute-start(bf16[8,128,128]{2,1,0:T(8,128)(2,1)S(1)} %get-tuple-element.37), channel_id=1, source_target_pairs={{0,16},{8,24},{16,0},{24,8},{1,17},{9,25},{17,1},{25,9},{2,18},{10... | collective-permute-start | bytes 786440 | tf_op jit(solution)/shard_map/ppermute | solution.py:215
  30.1 11.6 %collective-permute-start.15 = (bf16[8,128,128]{2,1,0:T(8,128)(2,1)S(1)}, bf16[8,128,128]{2,1,0:T(8,128)(2,1)S(1)}, u32[]{:S(2)}, u32[]{:S(2)}) collective-permute-start(bf16[8,128,128]{2,1,0:T(8,128)(2,1)S(1)} %get-tuple-element.38), channel_id=1, source_target_pairs={{0,24},{8,16},{16,8},{24,0},{1,25},{9,17},{17,9},{25,1},{2,26},{10... | collective-permute-start | bytes 786440 | tf_op jit(solution)/shard_map/ppermute | solution.py:215
  36.1 19.0 %collective-permute-start.12 = (bf16[192,1024]{1,0:T(8,128)(2,1)S(1)}, bf16[192,1024]{1,0:T(8,128)(2,1)S(1)}, u32[]{:S(2)}, u32[]{:S(2)}) collective-permute-start(bf16[192,1024]{1,0:T(8,128)(2,1)S(1)} %add_convert_fusion.1), channel_id=1, source_target_pairs={{0,4},{1,5},{2,6},{3,7},{4,0},{5,1},{6,2},{7,3},{8,12},{9,13},{10,... | collective-permute-start | bytes 1179656 | tf_op jit(solution)/shard_map/ppermute | solution.py:218

commit v3 on v2

--- a/solution.py
+++ b/solution.py
@@ -155,6 +155,11 @@
     for k in range(n_z):
         mine[k][...] = out[k]
         other[k][...] = out[n_z + k]
+
+
+def relay_kernel(cross, passed, a, b, both, near):
+    both[...] = (cross[...].astype(F32) + passed[...].astype(F32)).astype(BF16)
+    near[...] = (a[...].astype(F32) + b[...].astype(F32)).astype(BF16)
 
 
 def add_kernel(a, b, out):
@@ -193,8 +198,9 @@
 def grad_kernel(n_f, held, after, xs, dys, dps, hs, *outs):
     for s in range(n_f * held):
         f, i = s // held, s % held
-        outs[f][i] = dot(xs[s], dps[s], ((0,), (0,))).astype(BF16)
-        outs[f][held + i] = dot(hs[s], dys[s], ((0,), (0,))).astype(BF16)
+        out, i = (outs[f % 2], f // 2 * 2 * held + i) if n_f == 4 else (outs[f], i)
+        out[i] = dot(xs[s], dps[s], ((0,), (0,))).astype(BF16)
+        out[held + i] = dot(hs[s], dys[s], ((0,), (0,))).astype(BF16)
 
 
 def on_device(inputs, cotangent, up_tiles, up_rows, up_cols, down_tiles, down_rows, down_cols):
@@ -229,12 +235,12 @@
     )(*where, up)
     x_v, dy_v = pl.pallas_call(
         fetch_kernel,
-        out_shape=[jax.ShapeDtypeStruct(inputs.shape, BF16)] * 2,
+        out_shape=[pltpu.VMEM(inputs.shape, BF16)] * 2,
         in_specs=[HBM, HBM],
         out_specs=[VMEM, VMEM],
         scratch_shapes=[pltpu.SemaphoreType.DMA((2,))],
         compiler_params=vmem_limit(16),
-    )(inputs, cotangent)
+    )(*(pltpu.with_memory_space_constraint(a, pltpu.HBM) for a in (inputs, cotangent)))
     ups = [over_f(sent, k) for k in range(1, n_f)]
     tiles = [sent] + ups + [down] + downs
     outs = main_call(
@@ -242,15 +248,31 @@
     )
     mine, other = outs[:n_z], outs[n_z : 2 * n_z]
     chosen = outs[2 * n_z :]
-    parts = [
-        (m.astype(F32) + over_t(o, 1).astype(F32)).astype(BF16)
-        for m, o in zip(mine, other)
-    ]
+    def joined(q, lo=0, hi=None):
+        a, b = mine[q][:, lo:hi], theirs[q][:, lo:hi]
+        return (a.astype(F32) + b.astype(F32)).astype(BF16)
+
+    theirs = [over_t(o, 1) for o in other]
     if n_z == 4:
-        far, cross, near, own = parts
-        passed = over_t(far, 2)
+        cut = per_dev * TILE * 5 // 8
+        op_a = joined(0, 0, cut)
+        passed = over_t(op_a, 2)
+        op_b = joined(0, cut)
+        passed2 = over_t(op_b, 2)
+        across = over_t((joined(1, 0, cut).astype(F32) + passed.astype(F32)).astype(BF16), 4)
+        both, near = pl.pallas_call(
+            relay_kernel,
+            out_shape=[
+                jax.ShapeDtypeStruct(passed2.shape, BF16),
+                jax.ShapeDtypeStruct(mine[2].shape, BF16),
+            ],
+            in_specs=[VMEM] * 4,
+            out_specs=[VMEM] * 2,
+            compiler_params=vmem_limit(8),
+        )(joined(1, cut), passed2, mine[2], theirs[2])
+        across2 = over_t(both, 4)
         came = over_t(near, 2)
-        across = over_t((cross.astype(F32) + passed.astype(F32)).astype(BF16), 4)
+        own = joined(3)
         acc = pl.pallas_call(
             add_kernel,
             out_shape=jax.ShapeDtypeStruct(own.shape, F32),
@@ -258,27 +280,34 @@
             out_specs=VMEM,
             compiler_params=vmem_limit(8),
         )(own, came)
-        input_grad = (acc + across.astype(F32)).astype(BF16)
-        gate = near
+        input_grad = jnp.concatenate(
+            [(acc[:, :cut] + across.astype(F32)).astype(BF16), (acc[:, cut:] + across2.astype(F32)).astype(BF16)], axis=1
+        )
+        gate = op_a
     else:
         input_grad = lax.psum_scatter(
-            jnp.stack(parts),
+            jnp.stack([joined(q) for q in range(n_z)]),
             "tensor",
             scatter_dimension=0,
             tiled=False,
             axis_index_groups=[list(range(c, n_t, 2)) for c in range(2)],
         )
-        gate = parts[0]
+        gate = theirs[0]
+    sets = 2 if n_f == 4 else n_f
     terms = pl.pallas_call(
         functools.partial(grad_kernel, n_f, held),
-        out_shape=[jax.ShapeDtypeStruct((2 * held, TILE, TILE), BF16)] * n_f,
+        out_shape=[jax.ShapeDtypeStruct((n_f // sets * 2 * held, TILE, TILE), BF16)] * sets,
         in_specs=[ANY] + [VMEM] * 4,
-        out_specs=[VMEM] * n_f,
+        out_specs=[VMEM] * sets,
         compiler_params=vmem_limit(16),
     )(gate, *chosen)
-    total = terms[0].astype(F32)
-    for k in range(1, n_f):
-        total = total + over_f(terms[k], k).astype(F32)
+    if n_f == 4:
+        half = terms[0].astype(F32) + over_f(terms[1], 1).astype(F32)
+        total = half[: 2 * held] + over_f(half[2 * held :].astype(BF16), 2).astype(F32)
+    else:
+        total = terms[0].astype(F32)
+        for k in range(1, n_f):
+            total = total + over_f(terms[k], k).astype(F32)
     total = total.astype(BF16)
     return (input_grad, total[:held][None], total[held:][None])
 

time: 56.2 us -> 53.8 us (0.957)
  local copies, waits for them, and re-layouts: 4.5 us -> 0.76 us
  waiting for transfers between devices: 23.9 us -> 20.7 us
  Pallas kernels: 7.62 us -> 10.1 us
  starting transfers between devices: 17.5 us -> 19.7 us
    unnamed x8 -> x4, local copies, waits for them, and re-layouts: 3.79 us -> 0.01 us
    ppermute x7 -> x9, starting transfers between devices: 5.86 us -> 8.67 us  [over_t(): return lax.ppermute(a, 'tensor', [(i, i ^ k) for i in range(n_t)])]
    pallas_call x1 -> x2, Pallas kernels: 0.44 us -> 3.02 us  [the longest x1 2.9 us: on_device(): pl.pallas_call(fetch_kernel, out_shape=[pltpu.VMEM(inputs.shape, BF16)] *...]
    ppermute x7 -> x9, waiting for transfers between devices: 18.3 us -> 16.2 us  [over_t(): return lax.ppermute(a, 'tensor', [(i, i ^ k) for i in range(n_t)])]
    ppermute x9 -> x8, waiting for transfers between devices: 5.59 us -> 4.46 us  [over_f(): return lax.ppermute(a, 'fsdp', [(f, f ^ k) for f in range(n_f)])]
    convert_element_type x5 -> x7, other arithmetic: 1.42 us -> 0.54 us  [the longest x4 0.33 us: joined(): return (a.astype(F32) + b.astype(F32)).astype(BF16)]
    concatenate x0 -> x1, other arithmetic: none -> 0.8 us  [on_device(): jnp.concatenate([(acc[:, :cut] + across.astype(F32)).astype(BF16), (acc[:...]
    ppermute x9 -> x8, starting transfers between devices: 11.6 us -> 11 us  [over_f(): return lax.ppermute(a, 'fsdp', [(f, f ^ k) for f in range(n_f)])]
  transfers between devices with their start and end apart: 16 -> 17, of which waited for: 6 -> 6; matrix products, arithmetic and copies ran while one was open for 3% -> 3% of each run, Pallas kernels for 5% -> 10%
where the time goes in v3:
time: 53.8 us; the launch traced here: 53.6 us
  waiting for transfers between devices  20.7 us (38%)
  starting transfers between devices  19.7 us (37%)
  Pallas kernels  10.1 us (19%)
  other arithmetic  1.6 us (3%)
  between operations  0.79 us (1%)
  local copies, waits for them, and re-layouts  0.76 us (1%)
    ppermute x9, waiting for transfers between devices, over_t(): return lax.ppermute(a, 'tensor', [(i, i ^ k) for i in range(n_t)])  16.2 us
    ppermute x8, starting transfers between devices, over_f(): return lax.ppermute(a, 'fsdp', [(f, f ^ k) for f in range(n_f)])  11 us
    ppermute x9, starting transfers between devices, over_t(): return lax.ppermute(a, 'tensor', [(i, i ^ k) for i in range(n_t)])  8.67 us
    pallas_call x1, Pallas kernels, main_call(): pl.pallas_call(functools.partial(main_kernel, n_f, held, n_z, per_dev), o...  4.62 us
    ppermute x8, waiting for transfers between devices, over_f(): return lax.ppermute(a, 'fsdp', [(f, f ^ k) for f in range(n_f)])  4.46 us
    pallas_call x1, Pallas kernels, on_device(): pl.pallas_call(fetch_kernel, out_shape=[pltpu.VMEM(inputs.shape, BF16)] *...  2.9 us
    pallas_call x1, Pallas kernels, on_device(): pl.pallas_call(pack_kernel, out_shape=packed, in_specs=[SMEM] * 4 + [VMEM...  1.59 us
  transfers between devices with their start and end apart: 17, of which 6 were waited for; matrix products, arithmetic and copies ran while one was open for 3% of the time, Pallas kernels for 10%

profile of v3, /device:TPU:0, one launch (start us, length us, event | category | flops | bytes accessed | tf_op | source)
XLA Modules:
  0.0 53.6 jit_solution(7189964377086804485)
XLA Ops:
  0.6 4.0 %collective-permute-start.5 = (bf16[4,128,128]{2,1,0:T(8,128)(2,1)}, bf16[4,128,128]{2,1,0:T(8,128)(2,1)S(1)}, u32[]{:S(2)}, u32[]{:S(2)}) collective-permute-start(bf16[4,128,128]{2,1,0:T(8,128)(2,1)} %bitcast.8), channel_id=1, source_target_pairs={{0,24},{8,16},{16,8},{24,0},{1,25},{9,17},{17,9},{25,1},{2,26},{10... | collective-permute-start | bytes 393224 | tf_op jit(solution)/shard_map/ppermute | solution.py:221
  4.6 1.6 %shard_map.104.refs_0_ = bf16[528,128]{1,0:T(8,128)(2,1)} custom-call(s32[1,4]{1,0:T(1,128)} %ur.1, s32[1,4]{1,0:T(1,128)} %uc.1, s32[1,4]{1,0:T(1,128)} %dr.1, s32[1,4]{1,0:T(1,128)} %dc.1, bf16[4,128,128]{2,1,0:T(8,128)(2,1)} %bitcast.12), custom_call_target="tpu_custom_call" | custom-call | tf_op jit(solution)/shard_map/pallas_call | solution.py:230
  6.2 0.0 collective-permute-start.2
  6.2 2.0 %collective-permute-start.1 = (bf16[528,128]{1,0:T(8,128)(2,1)}, bf16[528,128]{1,0:T(8,128)(2,1)S(1)}, u32[]{:S(2)}, u32[]{:S(2)}) collective-permute-start(bf16[528,128]{1,0:T(8,128)(2,1)} %shard_map.104.refs_0_), channel_id=1, source_target_pairs={{0,16},{8,24},{16,0},{24,8},{1,17},{9,25},{17,1},{25,9},{2,18},{10... | collective-permute-start | bytes 405512 | tf_op jit(solution)/shard_map/ppermute | solution.py:221
  8.2 1.5 %collective-permute-start = (bf16[528,128]{1,0:T(8,128)(2,1)}, bf16[528,128]{1,0:T(8,128)(2,1)S(1)}, u32[]{:S(2)}, u32[]{:S(2)}) collective-permute-start(bf16[528,128]{1,0:T(8,128)(2,1)} %shard_map.104.refs_0_), channel_id=1, source_target_pairs={{0,8},{8,0},{16,24},{24,16},{1,9},{9,1},{17,25},{25,17},{2,10},{10... | collective-permute-start | bytes 405512 | tf_op jit(solution)/shard_map/ppermute | solution.py:221
  9.7 0.5 collective-permute-start.4
  10.2 0.0 collective-permute-done.5.refs_7_
  10.2 0.1 collective-permute-start.3
  10.3 0.0 copy-start
  10.3 0.0 copy-start.1
  10.3 2.9 %shard_map.103 = (bf16[192,8192]{1,0:T(8,128)(2,1)S(1)}, bf16[192,8192]{1,0:T(8,128)(2,1)S(1)}) custom-call(bf16[192,8192]{1,0:T(8,128)(2,1)} %x.1, bf16[192,8192]{1,0:T(8,128)(2,1)} %dy.1), custom_call_target="tpu_custom_call" | custom-call | tf_op jit(solution)/shard_map/pallas_call | solution.py:236
  13.2 0.1 pad_add_fusion.z_ref
  13.2 3.9 %collective-permute-done.4.refs_6_ = bf16[4,128,128]{2,1,0:T(8,128)(2,1)S(1)} collective-permute-done((bf16[4,128,128]{2,1,0:T(8,128)(2,1)}, bf16[4,128,128]{2,1,0:T(8,128)(2,1)S(1)}, u32[]{:S(2)}, u32[]{:S(2)}) %collective-permute-start.4) | collective-permute-done | bytes 131104 | tf_op jit(solution)/shard_map/ppermute | solution.py:221
  17.2 0.0 collective-permute-done.3.refs_5_
  17.2 0.0 collective-permute-done.2.refs_3_
  17.2 0.0 collective-permute-done.1.refs_2_
  17.2 0.0 collective-permute-done.refs_1_
  17.2 0.0 copy-done
  17.2 0.0 copy-done.1
  17.2 4.6 %shard_map.105 = (bf16[192,1024]{1,0:T(8,128)(2,1)S(1)}, bf16[192,1024]{1,0:T(8,128)(2,1)S(1)}, bf16[192,1024]{1,0:T(8,128)(2,1)S(1)}, bf16[192,1024]{1,0:T(8,12...) custom-call(s32[2]{0:T(128)S(1)} %pad_add_fusion.z_ref, ...), custom_call_target="tpu_custom_call" | custom-call | tf_op jit(solution)/shard_map/pallas_call | solution.py:174
  21.9 0.1 collective-permute-start.8
  21.9 0.5 collective-permute-start.6
  22.4 0.1 collective-permute-start.7
  22.5 0.4 collective-permute-start.10
  22.9 0.7 %collective-permute-done.8 = bf16[192,1024]{1,0:T(8,128)(2,1)S(1)} collective-permute-done((bf16[192,1024]{1,0:T(8,128)(2,1)S(1)}, bf16[192,1024]{1,0:T(8,128)(2,1)S(1)}, u32[]{:S(2)}, u32[]{:S(2)}) %collective-permute-start.8) | collective-permute-done | bytes 393248 | tf_op jit(solution)/shard_map/ppermute | solution.py:224
  23.6 0.1 add_convert_fusion.4
  23.7 1.9 %collective-permute-start.9 = (bf16[192,384]{1,0:T(8,128)(2,1)S(1)}, bf16[192,384]{1,0:T(8,128)(2,1)S(1)}, u32[]{:S(2)}, u32[]{:S(2)}) collective-permute-start(bf16[192,384]{1,0:T(8,128)(2,1)S(1)} %add_convert_fusion.4), channel_id=1, source_target_pairs={{0,2},{1,3},{2,0},{3,1},{4,6},{5,7},{6,4},{7,5},{8,10},{9,11},{10,... | collective-permute-start | bytes 442376 | tf_op jit(solution)/shard_map/ppermute | solution.py:224
  25.6 0.1 add_convert_fusion.2.after
  25.7 0.3 collective-permute-start.12
  26.0 0.8 %shard_map.108 = (bf16[16,128,128]{2,1,0:T(8,128)(2,1)S(1)}, bf16[16,128,128]{2,1,0:T(8,128)(2,1)S(1)}) custom-call(bf16[192,640]{1,0:T(8,128)(2,1)S(1)} %add_convert_fusion.2.after, bf16[16,192,128]{2,1,0:T(8,128)(2,1)S(1)} %get-tuple-element.33.xs, bf16[16,192,128]{2,1,0:T(8,128)(2,1)S(1)} %get-tuple-element.34.dys, ...), custom_call_target="tpu_custom_call" | custom-call | tf_op jit(solution)/shard_map/pallas_call | solution.py:297
  26.7 0.0 collective-permute-done.6
  26.7 1.5 %collective-permute-start.15 = (bf16[16,128,128]{2,1,0:T(8,128)(2,1)S(1)}, bf16[16,128,128]{2,1,0:T(8,128)(2,1)S(1)}, u32[]{:S(2)}, u32[]{:S(2)}) collective-permute-start(bf16[16,128,128]{2,1,0:T(8,128)(2,1)S(1)} %get-tuple-element.38), channel_id=1, source_target_pairs={{0,8},{8,0},{16,24},{24,16},{1,9},{9,1},{17,25},{25,17},{2,10},{10... | collective-permute-start | bytes 1572872 | tf_op jit(solution)/shard_map/ppermute | solution.py:221
  28.3 0.1 add_convert_fusion.a
  28.4 0.0 collective-permute-done.7
  28.4 0.1 add_convert_fusion.5.cross
  28.5 0.0 collective-permute-done.10.b
  28.5 2.0 %collective-permute-done.9.passed = bf16[192,384]{1,0:T(8,128)(2,1)S(1)} collective-permute-done((bf16[192,384]{1,0:T(8,128)(2,1)S(1)}, bf16[192,384]{1,0:T(8,128)(2,1)S(1)}, u32[]{:S(2)}, u32[]{:S(2)}) %collective-permute-start.9) | collective-permute-done | bytes 147488 | tf_op jit(solution)/shard_map/ppermute | solution.py:224
  30.5 0.1 shard_map.106
  30.6 2.7 %collective-permute-start.14 = (bf16[192,384]{1,0:T(8,128)(2,1)S(1)}, bf16[192,384]{1,0:T(8,128)(2,1)S(1)}, u32[]{:S(2)}, u32[]{:S(2)}) collective-permute-start(bf16[192,384]{1,0:T(8,128)(2,1)S(1)} %get-tuple-element.32), channel_id=1, source_target_pairs={{0,4},{1,5},{2,6},{3,7},{4,0},{5,1},{6,2},{7,3},{8,12},{9,13},{10,... | collective-permute-start | bytes 442376 | tf_op jit(solution)/shard_map/ppermute | solution.py:224
  33.3 1.9 %collective-permute-start.11 = (bf16[192,1024]{1,0:T(8,128)(2,1)S(1)}, bf16[192,1024]{1,0:T(8,128)(2,1)S(1)}, u32[]{:S(2)}, u32[]{:S(2)}) collective-permute-start(bf16[192,1024]{1,0:T(8,128)(2,1)S(1)} %get-tuple-element.31), channel_id=1, source_target_pairs={{0,2},{1,3},{2,0},{3,1},{4,6},{5,7},{6,4},{7,5},{8,10},{9,11},{10,... | collective-permute-start | bytes 1179656 | tf_op jit(solution)/shard_map/ppermute | solution.py:224
  35.3 3.6 %collective-permute-done.12 = bf16[192,640]{1,0:T(8,128)(2,1)S(1)} collective-permute-done((bf16[192,640]{1,0:T(8,128)(2,1)S(1)}, bf16[192,640]{1,0:T(8,128)(2,1)S(1)}, u32[]{:S(2)}, u32[]{:S(2)}) %collective-permute-start.12) | collective-permute-done | bytes 245792 | tf_op jit(solution)/shard_map/ppermute | solution.py:224
  38.9 0.1 add_convert_fusion.1
  39.0 0.8 %collective-permute-start.13 = (bf16[192,640]{1,0:T(8,128)(2,1)S(1)}, bf16[192,640]{1,0:T(8,128)(2,1)S(1)}, u32[]{:S(2)}, u32[]{:S(2)}) collective-permute-start(bf16[192,640]{1,0:T(8,128)(2,1)S(1)} %add_convert_fusion.1), channel_id=1, source_target_pairs={{0,4},{1,5},{2,6},{3,7},{4,0},{5,1},{6,2},{7,3},{8,12},{9,13},{10,... | collective-permute-start | bytes 737288 | tf_op jit(solution)/shard_map/ppermute | solution.py:224
  39.8 0.5 collective-permute-done.15
  40.3 0.1 convert_add_fusion
  40.5 1.5 %collective-permute-start.16 = (bf16[8,128,128]{2,1,0:T(8,128)(2,1)S(1)}, bf16[8,128,128]{2,1,0:T(8,128)(2,1)S(1)}, u32[]{:S(2)}, u32[]{:S(2)}) collective-permute-start(bf16[8,128,128]{2,1,0:T(8,128)(2,1)S(1)} %slice.87), channel_id=1, source_target_pairs={{0,16},{8,24},{16,0},{24,8},{1,17},{9,25},{17,1},{25,9},{2,18},{10... | collective-permute-start | bytes 786440 | tf_op jit(solution)/shard_map/ppermute | solution.py:221
  41.9 9.9 %collective-permute-done.11.b = bf16[192,1024]{1,0:T(8,128)(2,1)S(1)} collective-permute-done((bf16[192,1024]{1,0:T(8,128)(2,1)S(1)}, bf16[192,1024]{1,0:T(8,128)(2,1)S(1)}, u32[]{:S(2)}, u32[]{:S(2)}) %collective-permute-start.11) | collective-permute-done | bytes 393248 | tf_op jit(solution)/shard_map/ppermute | solution.py:224
  51.8 0.1 shard_map.107
  51.9 0.0 collective-permute-done.13
  51.9 0.1 fusion.1
  52.0 0.0 collective-permute-done.14
  52.0 0.8 %pad_maximum_fusion = bf16[192,1024]{1,0:T(8,128)(2,1)} fusion(bf16[192,384]{1,0:T(8,128)(2,1)S(1)} %fusion.2, bf16[192,640]{1,0:T(8,128)(2,1)S(1)} %fusion.1), kind=kLoop, calls=%fused_computation.10 | loop fusion | flops 786432 | bytes 786432 | tf_op jit(solution)/shard_map/concatenate | solution.py:283
  52.8 0.0 collective-permute-done.16
  52.8 0.1 fusion
  52.9 0.7 %slice_bitcast_fusion = (bf16[1,4,128,128]{3,2,1,0:T(8,128)(2,1)}, bf16[1,4,128,128]{3,2,1,0:T(8,128)(2,1)}) fusion(bf16[8,128,128]{2,1,0:T(8,128)(2,1)S(1)} %fusion), kind=kLoop, calls=%fused_computation.15 | loop fusion | bytes 524288 | tf_op jit(solution)/shard_map/broadcast_in_dim | solution.py:312
  (2 shorter events, 0.1 us)
Async XLA Ops:
  0.6 9.5 %collective-permute-start.5 = (bf16[4,128,128]{2,1,0:T(8,128)(2,1)}, bf16[4,128,128]{2,1,0:T(8,128)(2,1)S(1)}, u32[]{:S(2)}, u32[]{:S(2)}) collective-permute-start(bf16[4,128,128]{2,1,0:T(8,128)(2,1)} %bitcast.8), channel_id=1, source_target_pairs={{0,24},{8,16},{16,8},{24,0},{1,25},{9,17},{17,9},{25,1},{2,26},{10... | collective-permute-start | bytes 393224 | tf_op jit(solution)/shard_map/ppermute | solution.py:221
  6.2 11.0 %collective-permute-start.2 = (bf16[528,128]{1,0:T(8,128)(2,1)}, bf16[528,128]{1,0:T(8,128)(2,1)S(1)}, u32[]{:S(2)}, u32[]{:S(2)}) collective-permute-start(bf16[528,128]{1,0:T(8,128)(2,1)} %shard_map.104.refs_0_), channel_id=1, source_target_pairs={{0,24},{8,16},{16,8},{24,0},{1,25},{9,17},{17,9},{25,1},{2,26},{10... | collective-permute-start | bytes 405512 | tf_op jit(solution)/shard_map/ppermute | solution.py:221
  6.2 11.0 %collective-permute-start.1 = (bf16[528,128]{1,0:T(8,128)(2,1)}, bf16[528,128]{1,0:T(8,128)(2,1)S(1)}, u32[]{:S(2)}, u32[]{:S(2)}) collective-permute-start(bf16[528,128]{1,0:T(8,128)(2,1)} %shard_map.104.refs_0_), channel_id=1, source_target_pairs={{0,16},{8,24},{16,0},{24,8},{1,17},{9,25},{17,1},{25,9},{2,18},{10... | collective-permute-start | bytes 405512 | tf_op jit(solution)/shard_map/ppermute | solution.py:221
  8.2 9.0 %collective-permute-start = (bf16[528,128]{1,0:T(8,128)(2,1)}, bf16[528,128]{1,0:T(8,128)(2,1)S(1)}, u32[]{:S(2)}, u32[]{:S(2)}) collective-permute-start(bf16[528,128]{1,0:T(8,128)(2,1)} %shard_map.104.refs_0_), channel_id=1, source_target_pairs={{0,8},{8,0},{16,24},{24,16},{1,9},{9,1},{17,25},{25,17},{2,10},{10... | collective-permute-start | bytes 405512 | tf_op jit(solution)/shard_map/ppermute | solution.py:221
  9.7 7.5 %collective-permute-start.4 = (bf16[4,128,128]{2,1,0:T(8,128)(2,1)}, bf16[4,128,128]{2,1,0:T(8,128)(2,1)S(1)}, u32[]{:S(2)}, u32[]{:S(2)}) collective-permute-start(bf16[4,128,128]{2,1,0:T(8,128)(2,1)} %bitcast.9), channel_id=1, source_target_pairs={{0,16},{8,24},{16,0},{24,8},{1,17},{9,25},{17,1},{25,9},{2,18},{10... | collective-permute-start | bytes 393224 | tf_op jit(solution)/shard_map/ppermute | solution.py:221
  10.2 7.0 %collective-permute-start.3 = (bf16[4,128,128]{2,1,0:T(8,128)(2,1)}, bf16[4,128,128]{2,1,0:T(8,128)(2,1)S(1)}, u32[]{:S(2)}, u32[]{:S(2)}) collective-permute-start(bf16[4,128,128]{2,1,0:T(8,128)(2,1)} %bitcast.10), channel_id=1, source_target_pairs={{0,8},{8,0},{16,24},{24,16},{1,9},{9,1},{17,25},{25,17},{2,10},{10... | collective-permute-start | bytes 393224 | tf_op jit(solution)/shard_map/ppermute | solution.py:221
  10.3 7.0 %copy-start = (bf16[528,128]{1,0:T(8,128)(2,1)S(1)}, bf16[528,128]{1,0:T(8,128)(2,1)}, u32[]{:S(2)}) copy-start(bf16[528,128]{1,0:T(8,128)(2,1)} %shard_map.104.refs_0_) | copy-start | bytes 405508
  10.3 7.0 %copy-start.1 = (bf16[1,4,128,128]{3,2,1,0:T(8,128)(2,1)S(1)}, bf16[1,4,128,128]{3,2,1,0:T(8,128)(2,1)}, u32[]{:S(2)}) copy-start(bf16[1,4,128,128]{3,2,1,0:T(8,128)(2,1)} %param.13) | copy-start | bytes 393220
  21.9 1.8 %collective-permute-start.8 = (bf16[192,1024]{1,0:T(8,128)(2,1)S(1)}, bf16[192,1024]{1,0:T(8,128)(2,1)S(1)}, u32[]{:S(2)}, u32[]{:S(2)}) collective-permute-start(bf16[192,1024]{1,0:T(8,128)(2,1)S(1)} %get-tuple-element.28), channel_id=1, source_target_pairs={{0,1},{1,0},{2,3},{3,2},{4,5},{5,4},{6,7},{7,6},{8,9},{9,8},{10,11... | collective-permute-start | bytes 1179656 | tf_op jit(solution)/shard_map/ppermute | solution.py:224
  21.9 4.8 %collective-permute-start.6 = (bf16[192,1024]{1,0:T(8,128)(2,1)S(1)}, bf16[192,1024]{1,0:T(8,128)(2,1)S(1)}, u32[]{:S(2)}, u32[]{:S(2)}) collective-permute-start(bf16[192,1024]{1,0:T(8,128)(2,1)S(1)} %get-tuple-element.24), channel_id=1, source_target_pairs={{0,1},{1,0},{2,3},{3,2},{4,5},{5,4},{6,7},{7,6},{8,9},{9,8},{10,11... | collective-permute-start | bytes 1179656 | tf_op jit(solution)/shard_map/ppermute | solution.py:224
  22.4 6.0 %collective-permute-start.7 = (bf16[192,1024]{1,0:T(8,128)(2,1)S(1)}, bf16[192,1024]{1,0:T(8,128)(2,1)S(1)}, u32[]{:S(2)}, u32[]{:S(2)}) collective-permute-start(bf16[192,1024]{1,0:T(8,128)(2,1)S(1)} %get-tuple-element.26), channel_id=1, source_target_pairs={{0,1},{1,0},{2,3},{3,2},{4,5},{5,4},{6,7},{7,6},{8,9},{9,8},{10,11... | collective-permute-start | bytes 1179656 | tf_op jit(solution)/shard_map/ppermute | solution.py:224
  22.5 6.0 %collective-permute-start.10 = (bf16[192,1024]{1,0:T(8,128)(2,1)S(1)}, bf16[192,1024]{1,0:T(8,128)(2,1)S(1)}, u32[]{:S(2)}, u32[]{:S(2)}) collective-permute-start(bf16[192,1024]{1,0:T(8,128)(2,1)S(1)} %get-tuple-element.30), channel_id=1, source_target_pairs={{0,1},{1,0},{2,3},{3,2},{4,5},{5,4},{6,7},{7,6},{8,9},{9,8},{10,11... | collective-permute-start | bytes 1179656 | tf_op jit(solution)/shard_map/ppermute | solution.py:224
  23.7 6.8 %collective-permute-start.9 = (bf16[192,384]{1,0:T(8,128)(2,1)S(1)}, bf16[192,384]{1,0:T(8,128)(2,1)S(1)}, u32[]{:S(2)}, u32[]{:S(2)}) collective-permute-start(bf16[192,384]{1,0:T(8,128)(2,1)S(1)} %add_convert_fusion.4), channel_id=1, source_target_pairs={{0,2},{1,3},{2,0},{3,1},{4,6},{5,7},{6,4},{7,5},{8,10},{9,11},{10,... | collective-permute-start | bytes 442376 | tf_op jit(solution)/shard_map/ppermute | solution.py:224
  25.7 13.2 %collective-permute-start.12 = (bf16[192,640]{1,0:T(8,128)(2,1)S(1)}, bf16[192,640]{1,0:T(8,128)(2,1)S(1)}, u32[]{:S(2)}, u32[]{:S(2)}) collective-permute-start(bf16[192,640]{1,0:T(8,128)(2,1)S(1)} %add_convert_fusion.2.after), channel_id=1, source_target_pairs={{0,2},{1,3},{2,0},{3,1},{4,6},{5,7},{6,4},{7,5},{8,10},{9,11},{10,... | collective-permute-start | bytes 737288 | tf_op jit(solution)/shard_map/ppermute | solution.py:224
  26.7 13.5 %collective-permute-start.15 = (bf16[16,128,128]{2,1,0:T(8,128)(2,1)S(1)}, bf16[16,128,128]{2,1,0:T(8,128)(2,1)S(1)}, u32[]{:S(2)}, u32[]{:S(2)}) collective-permute-start(bf16[16,128,128]{2,1,0:T(8,128)(2,1)S(1)} %get-tuple-element.38), channel_id=1, source_target_pairs={{0,8},{8,0},{16,24},{24,16},{1,9},{9,1},{17,25},{25,17},{2,10},{10... | collective-permute-start | bytes 1572872 | tf_op jit(solution)/shard_map/ppermute | solution.py:221
  30.6 21.4 %collective-permute-start.14 = (bf16[192,384]{1,0:T(8,128)(2,1)S(1)}, bf16[192,384]{1,0:T(8,128)(2,1)S(1)}, u32[]{:S(2)}, u32[]{:S(2)}) collective-permute-start(bf16[192,384]{1,0:T(8,128)(2,1)S(1)} %get-tuple-element.32), channel_id=1, source_target_pairs={{0,4},{1,5},{2,6},{3,7},{4,0},{5,1},{6,2},{7,3},{8,12},{9,13},{10,... | collective-permute-start | bytes 442376 | tf_op jit(solution)/shard_map/ppermute | solution.py:224
  33.3 18.5 %collective-permute-start.11 = (bf16[192,1024]{1,0:T(8,128)(2,1)S(1)}, bf16[192,1024]{1,0:T(8,128)(2,1)S(1)}, u32[]{:S(2)}, u32[]{:S(2)}) collective-permute-start(bf16[192,1024]{1,0:T(8,128)(2,1)S(1)} %get-tuple-element.31), channel_id=1, source_target_pairs={{0,2},{1,3},{2,0},{3,1},{4,6},{5,7},{6,4},{7,5},{8,10},{9,11},{10,... | collective-permute-start | bytes 1179656 | tf_op jit(solution)/shard_map/ppermute | solution.py:224
  39.0 12.9 %collective-permute-start.13 = (bf16[192,640]{1,0:T(8,128)(2,1)S(1)}, bf16[192,640]{1,0:T(8,128)(2,1)S(1)}, u32[]{:S(2)}, u32[]{:S(2)}) collective-permute-start(bf16[192,640]{1,0:T(8,128)(2,1)S(1)} %add_convert_fusion.1), channel_id=1, source_target_pairs={{0,4},{1,5},{2,6},{3,7},{4,0},{5,1},{6,2},{7,3},{8,12},{9,13},{10,... | collective-permute-start | bytes 737288 | tf_op jit(solution)/shard_map/ppermute | solution.py:224
  40.5 12.4 %collective-permute-start.16 = (bf16[8,128,128]{2,1,0:T(8,128)(2,1)S(1)}, bf16[8,128,128]{2,1,0:T(8,128)(2,1)S(1)}, u32[]{:S(2)}, u32[]{:S(2)}) collective-permute-start(bf16[8,128,128]{2,1,0:T(8,128)(2,1)S(1)} %slice.87), channel_id=1, source_target_pairs={{0,16},{8,24},{16,0},{24,8},{1,17},{9,25},{17,1},{25,9},{2,18},{10... | collective-permute-start | bytes 786440 | tf_op jit(solution)/shard_map/ppermute | solution.py:221
